TPU v7x, 512 devices: a whole 4x8x8 slice. The times are simulated.
512 devices in a mesh: sub: 16 (over y_lo, x, core), tile: 32 (over z, y_hi).
Axes of the slice: x: 4, y: 8 (y_hi: 4, y_lo: 2; y = y_hi * 2 + y_lo), z: 8, core: 2. Of those that a mesh axis runs over, the one named last changes fastest.
Arguments:
- states: float32 [16, 3, 1024, 2048], P('sub', None, 'tile'), may hold values from -6 to 6
- terrain: int32 [1024, 2048], P('tile'), may hold values from 0 to 7
- depth_table: float32 [8], replicated, may hold values from 0.5 to 2
- spread_table: float32 [8], replicated, may hold values from 0.03 to 0.24
- mixing: float32 [16, 16], replicated, may hold values from -0.9 to 2, as said below
Outputs:
- gradient: float32 [16, 3, 1024, 2048], P('sub', None, 'tile')
Inputs may be any that keep to these rules, and one draw needn't show every extreme that they name: `mixing`: A dense matrix with diagonal entries between 1 and 2.
All inputs are finite; a program needn't handle non-finite values.
Results may differ from a plain program's by a relative error of at most 0.00012.
Values sent between devices are 32-bit elements; how exact they have to be, the bound alone decides.
No kernel may reach another device: no remote copies, remote signals or barrier semaphores. Data moves between devices by JAX's collectives and lax.ppermute only.
A program may use at most 64 MiB of HBM per device.

v0:
```python
import jax
import jax.numpy as jnp
from jax import lax
from jax.sharding import PartitionSpec as P

FSTEPS = 3
DSTEPS = 3


time_step = 0.5
gravity = 1.0
coriolis = 0.3


def with_halo(value, sides, width):
    for axis, dim in sides:
        peers, length = (lax.axis_size(axis), value.shape[dim])
        up = [(i, (i + 1) % peers) for i in range(peers - 1)]
        down = [(j, i) for i, j in up]
        last = lax.slice_in_dim(value, length - width, length, axis=dim)
        first = lax.slice_in_dim(value, 0, width, axis=dim)
        before = lax.ppermute(last, axis, up)
        after = lax.ppermute(first, axis, down)
        value = jnp.concatenate([before, value, after], axis=dim)
    return value


def passed_along(value, axis, by):
    peers = lax.axis_size(axis)
    pairs = [(i, i + by) for i in range(peers) if 0 <= i + by < peers]
    return lax.ppermute(value, axis, pairs)


def col_diff(field):
    return (jnp.roll(field, -1, -1) - jnp.roll(field, 1, -1)) * 0.5


def row_mask(first, count, total):
    index = first + jnp.arange(count, dtype=jnp.int32)
    return ((index >= 0) & (index < total)).astype(jnp.float32)[:, None]


def crop_rows(field, keep, have):
    cut = have - keep
    return field[cut : field.shape[0] - cut]


def model_step(state, depth, first, total):
    height, east, north = (state[0], state[1], state[2])
    flux_x = depth * east
    flux_y = depth * north
    new_h = height[1:-1] - time_step * ((flux_x[2:] - flux_x[:-2]) * 0.5 + col_diff(flux_y[1:-1]))
    new_h = new_h * row_mask(first + 1, new_h.shape[0], total)
    new_u = (
        east[2:-2]
        - time_step * gravity * (new_h[2:] - new_h[:-2]) * 0.5
        + time_step * coriolis * north[2:-2]
    )
    new_v = (
        north[2:-2]
        - time_step * gravity * col_diff(new_h[1:-1])
        - time_step * coriolis * east[2:-2]
    )
    result = jnp.stack([new_h[1:-1], new_u, new_v])
    return result * row_mask(first + 2, result.shape[1], total)


def spread_step(field, kappa, first, total):
    centre = field[:, 1:-1]
    laplace = (
        field[:, 2:]
        + field[:, :-2]
        + jnp.roll(centre, 1, 2)
        + jnp.roll(centre, -1, 2)
        - 4.0 * centre
    )
    return (centre + kappa * laplace) * row_mask(first + 1, centre.shape[1], total)


def local(states, terrain, depth_table, spread_table, mixing):
    state = states[0]
    rows = state.shape[1]
    total = rows * lax.axis_size("tile")
    anchor = lax.axis_index("tile") * rows
    classes = jnp.arange(depth_table.shape[0], dtype=jnp.int32)
    pick = (terrain[None] == classes[:, None, None]).astype(jnp.float32)
    coeffs = jnp.stack(
        [
            jnp.sum(pick * depth_table[:, None, None], 0),
            jnp.sum(pick * spread_table[:, None, None], 0),
        ]
    )
    wide = with_halo(coeffs, (("tile", 1),), 6)
    depth_wide = wide[0]
    kappa_wide = wide[1]
    for step in range(FSTEPS):
        padded = with_halo(state, (("tile", 1),), 2)
        state = model_step(padded, crop_rows(depth_wide, 2, 6), anchor - 2, total)
    earlier = passed_along(state, "sub", 1)
    jumps = states[0] - earlier
    mixed_parts = jnp.einsum(
        "st,tfxy->sfxy",
        mixing,
        lax.all_to_all(jumps[None], "sub", split_axis=3, concat_axis=0, tiled=True),
        precision=lax.Precision.HIGHEST,
    )
    mixed = lax.all_to_all(mixed_parts, "sub", split_axis=0, concat_axis=3, tiled=True)[0]
    field = mixed
    for step in range(DSTEPS):
        padded = with_halo(field, (("tile", 1),), 1)
        field = spread_step(padded, crop_rows(kappa_wide, 0, 6), anchor - 1, total)
    return field[None]


def solution(mesh):
    in_specs = (P("sub", None, "tile", None), P("tile", None), P(), P(), P())
    out_specs = P("sub", None, "tile", None)
    return jax.shard_map(local, mesh=mesh, in_specs=in_specs, out_specs=out_specs, check_vma=False)
```

profile of v0, /device:TPU:256, one launch (start us, length us, event | category | flops | bytes accessed | tf_op | source)
XLA Modules:
  0.0 192.1 jit_solution(10238110651382824811)
XLA Ops:
  1.1 4.5 %collective-permute-start = (f32[3,2,2048]{2,1,0:T(2,128)S(1)}, f32[3,2,2048]{2,1,0:T(2,128)S(1)}, u32[]{:S(2)}, u32[]{:S(2)}) collective-permute-start(f32[3,2,2048]{2,1,0:T(2,128)S(1)} %get-tuple-element.35), channel_id=1, source_target_pairs={{0,1},{1,2},{2,3},{3,4},{4,5},{5,6},{6,7},{7,8},{8,9},{9,10},{10,1... | collective-permute-start | bytes 147464 | tf_op jit(solution)/shard_map/ppermute | solution.py:22
  5.6 5.6 %collective-permute-start.1 = (f32[3,2,2048]{2,1,0:T(2,128)S(1)}, f32[3,2,2048]{2,1,0:T(2,128)S(1)}, u32[]{:S(2)}, u32[]{:S(2)}) collective-permute-start(f32[3,2,2048]{2,1,0:T(2,128)S(1)} %get-tuple-element.36), channel_id=1, source_target_pairs={{1,0},{2,1},{3,2},{4,3},{5,4},{6,5},{7,6},{8,7},{9,8},{10,9},{11,1... | collective-permute-start | bytes 147464 | tf_op jit(solution)/shard_map/ppermute | solution.py:23
  11.2 1.4 select_reduce_fusion.1
  12.8 1.9 %collective-permute-start.3 = (f32[2,6,2048]{2,0,1:T(2,128)S(1)}, f32[2,6,2048]{2,0,1:T(2,128)S(1)}, u32[]{:S(2)}, u32[]{:S(2)}) collective-permute-start(f32[2,6,2048]{2,0,1:T(2,128)S(1)} %copy.66), channel_id=1, source_target_pairs={{1,0},{2,1},{3,2},{4,3},{5,4},{6,5},{7,6},{8,7},{9,8},{10,9},{11,1... | collective-permute-start | bytes 294920 | tf_op jit(solution)/shard_map/ppermute | solution.py:23
  14.8 4.8 %collective-permute-start.2 = (f32[2,6,2048]{2,0,1:T(2,128)S(1)}, f32[2,6,2048]{2,0,1:T(2,128)S(1)}, u32[]{:S(2)}, u32[]{:S(2)}) collective-permute-start(f32[2,6,2048]{2,0,1:T(2,128)S(1)} %copy.65), channel_id=1, source_target_pairs={{0,1},{1,2},{2,3},{3,4},{4,5},{5,6},{6,7},{7,8},{8,9},{9,10},{10,1... | collective-permute-start | bytes 294920 | tf_op jit(solution)/shard_map/ppermute | solution.py:22
  19.8 1.5 collective-permute-done.3
  21.4 4.5 %collective-permute-done.2 = f32[2,6,2048]{2,0,1:T(2,128)S(1)} collective-permute-done((f32[2,6,2048]{2,0,1:T(2,128)S(1)}, f32[2,6,2048]{2,0,1:T(2,128)S(1)}, u32[]{:S(2)}, u32[]{:S(2)}) %collective-permute-start.2) | collective-permute-done | bytes 98336 | tf_op jit(solution)/shard_map/ppermute | solution.py:22
  27.2 2.0 %collective-permute-start.4 = (f32[3,2,2048]{2,1,0:T(2,128)S(1)}, f32[3,2,2048]{2,1,0:T(2,128)S(1)}, u32[]{:S(2)}, u32[]{:S(2)}) collective-permute-start(f32[3,2,2048]{2,1,0:T(2,128)S(1)} %get-tuple-element.33), channel_id=1, source_target_pairs={{0,1},{1,2},{2,3},{3,4},{4,5},{5,6},{6,7},{7,8},{8,9},{9,10},{10,1... | collective-permute-start | bytes 147464 | tf_op jit(solution)/shard_map/ppermute | solution.py:22
  29.2 8.1 %collective-permute-start.5 = (f32[3,2,2048]{2,1,0:T(2,128)S(1)}, f32[3,2,2048]{2,1,0:T(2,128)S(1)}, u32[]{:S(2)}, u32[]{:S(2)}) collective-permute-start(f32[3,2,2048]{2,1,0:T(2,128)S(1)} %get-tuple-element.34), channel_id=1, source_target_pairs={{1,0},{2,1},{3,2},{4,3},{5,4},{6,5},{7,6},{8,7},{9,8},{10,9},{11,1... | collective-permute-start | bytes 147464 | tf_op jit(solution)/shard_map/ppermute | solution.py:23
  37.4 2.0 %collective-permute-done.5 = f32[3,2,2048]{2,1,0:T(2,128)S(1)} collective-permute-done((f32[3,2,2048]{2,1,0:T(2,128)S(1)}, f32[3,2,2048]{2,1,0:T(2,128)S(1)}, u32[]{:S(2)}, u32[]{:S(2)}) %collective-permute-start.5) | collective-permute-done | bytes 49184 | tf_op jit(solution)/shard_map/ppermute | solution.py:23
  40.7 3.2 %collective-permute-start.6 = (f32[3,2,2048]{2,1,0:T(2,128)S(1)}, f32[3,2,2048]{2,1,0:T(2,128)S(1)}, u32[]{:S(2)}, u32[]{:S(2)}) collective-permute-start(f32[3,2,2048]{2,1,0:T(2,128)S(1)} %get-tuple-element.31), channel_id=1, source_target_pairs={{0,1},{1,2},{2,3},{3,4},{4,5},{5,6},{6,7},{7,8},{8,9},{9,10},{10,1... | collective-permute-start | bytes 147464 | tf_op jit(solution)/shard_map/ppermute | solution.py:22
  43.9 7.3 %collective-permute-start.7 = (f32[3,2,2048]{2,1,0:T(2,128)S(1)}, f32[3,2,2048]{2,1,0:T(2,128)S(1)}, u32[]{:S(2)}, u32[]{:S(2)}) collective-permute-start(f32[3,2,2048]{2,1,0:T(2,128)S(1)} %get-tuple-element.32), channel_id=1, source_target_pairs={{1,0},{2,1},{3,2},{4,3},{5,4},{6,5},{7,6},{8,7},{9,8},{10,9},{11,1... | collective-permute-start | bytes 147464 | tf_op jit(solution)/shard_map/ppermute | solution.py:23
  54.1 1.3 collective-permute-start.8
  55.5 1.8 collective-permute-done.8
  58.3 6.9 %copy.60 = f32[1,3,32,2048]{2,0,1,3:T(1,128)S(1)} copy(f32[1,3,32,2048]{3,2,1,0:T(8,128)} %subtract_bitcast_fusion) | data formatting | bytes 1572864 | tf_op jit(solution)/shard_map/broadcast_in_dim | solution.py:104
  65.8 11.9 %reduce = f32[2048,3,32]{2,1,0:T(4,128)} reduce(f32[2048,3,1,32]{3,2,1,0:T(1,128)S(1)} %bitcast.132, f32[]{:T(128)} %broadcast.134), dimensions={2}, to_apply=%bitcast.130.reduce_sub_computation | reduce | bytes 1572868
  77.7 4.5 %reshape.264 = f32[16,1,12288]{2,1,0:T(1,128)S(1)} reshape(f32[2048,3,32]{2,1,0:T(4,128)} %reduce) | data formatting | bytes 1572864
  82.2 29.4 %all_to_all.33 = f32[16,1,12288]{2,1,0:T(1,128)S(1)} all-to-all(f32[16,1,12288]{2,1,0:T(1,128)S(1)} %reshape.264), channel_id=1, replica_groups=mesh['sub'=16,'tile'=32] {'sub'}, dimensions={0} | all-to-all | bytes 1572864 | tf_op jit(solution)/shard_map/all_to_all | solution.py:104
  111.6 3.6 %reduce.1 = f32[16,12288]{1,0:T(8,128)} reduce(f32[16,1,12288]{2,1,0:T(1,128)S(1)} %all_to_all.33, f32[]{:T(128)} %broadcast.134), dimensions={1}, to_apply=%all_to_all.24.reduce_sub_computation | reduce | bytes 1572868 | tf_op jit(solution)/shard_map/all_to_all | solution.py:104
  115.3 6.4 %reshape.265 = f32[2048,3,1,32]{3,2,1,0:T(1,128)S(1)} reshape(f32[16,12288]{1,0:T(8,128)} %reduce.1) | data formatting | bytes 1572864
  121.6 5.8 %copy.61 = f32[1,3,32,2048]{3,2,1,0:T(8,128)} copy(f32[1,3,32,2048]{2,0,1,3:T(1,128)S(1)} %bitcast.133) | data formatting | bytes 1572864 | tf_op jit(solution)/shard_map/all_to_all | solution.py:104
  129.8 16.3 %all_to_all.34 = f32[16,3,32,128]{3,2,1,0:T(8,128)S(1)} all-to-all(f32[16,3,32,128]{3,2,1,0:T(8,128)S(1)} %copy.62), channel_id=1, replica_groups=mesh['sub'=16,'tile'=32] {'sub'}, dimensions={0} | all-to-all | bytes 1572864 | tf_op jit(solution)/shard_map/all_to_all | solution.py:107
  147.0 8.5 %collective-permute-start.9 = (f32[3,1,2048]{2,1,0:T(1,128)S(1)}, f32[3,1,2048]{2,1,0:T(1,128)S(1)}, u32[]{:S(2)}, u32[]{:S(2)}) collective-permute-start(f32[3,1,2048]{2,1,0:T(1,128)S(1)} %get-tuple-element.29), channel_id=1, source_target_pairs={{1,0},{2,1},{3,2},{4,3},{5,4},{6,5},{7,6},{8,7},{9,8},{10,9},{11,1... | collective-permute-start | bytes 73736 | tf_op jit(solution)/shard_map/ppermute | solution.py:23
  155.5 1.9 %collective-permute-start.10 = (f32[3,1,2048]{2,1,0:T(1,128)S(1)}, f32[3,1,2048]{2,1,0:T(1,128)S(1)}, u32[]{:S(2)}, u32[]{:S(2)}) collective-permute-start(f32[3,1,2048]{2,1,0:T(1,128)S(1)} %get-tuple-element.30), channel_id=1, source_target_pairs={{0,1},{1,2},{2,3},{3,4},{4,5},{5,6},{6,7},{7,8},{8,9},{9,10},{10,1... | collective-permute-start | bytes 73736 | tf_op jit(solution)/shard_map/ppermute | solution.py:22
  157.5 7.9 %collective-permute-done.10 = f32[3,1,2048]{2,1,0:T(1,128)S(1)} collective-permute-done((f32[3,1,2048]{2,1,0:T(1,128)S(1)}, f32[3,1,2048]{2,1,0:T(1,128)S(1)}, u32[]{:S(2)}, u32[]{:S(2)}) %collective-permute-start.10) | collective-permute-done | bytes 24608 | tf_op jit(solution)/shard_map/ppermute | solution.py:22
  166.2 1.9 %collective-permute-start.11 = (f32[3,1,2048]{2,1,0:T(1,128)S(1)}, f32[3,1,2048]{2,1,0:T(1,128)S(1)}, u32[]{:S(2)}, u32[]{:S(2)}) collective-permute-start(f32[3,1,2048]{2,1,0:T(1,128)S(1)} %get-tuple-element.23), channel_id=1, source_target_pairs={{1,0},{2,1},{3,2},{4,3},{5,4},{6,5},{7,6},{8,7},{9,8},{10,9},{11,1... | collective-permute-start | bytes 73736 | tf_op jit(solution)/shard_map/ppermute | solution.py:23
  168.1 4.8 %collective-permute-start.12 = (f32[3,1,2048]{2,1,0:T(1,128)S(1)}, f32[3,1,2048]{2,1,0:T(1,128)S(1)}, u32[]{:S(2)}, u32[]{:S(2)}) collective-permute-start(f32[3,1,2048]{2,1,0:T(1,128)S(1)} %get-tuple-element.24), channel_id=1, source_target_pairs={{0,1},{1,2},{2,3},{3,4},{4,5},{5,6},{6,7},{7,8},{8,9},{9,10},{10,1... | collective-permute-start | bytes 73736 | tf_op jit(solution)/shard_map/ppermute | solution.py:22
  173.1 5.0 %collective-permute-done.12 = f32[3,1,2048]{2,1,0:T(1,128)S(1)} collective-permute-done((f32[3,1,2048]{2,1,0:T(1,128)S(1)}, f32[3,1,2048]{2,1,0:T(1,128)S(1)}, u32[]{:S(2)}, u32[]{:S(2)}) %collective-permute-start.12) | collective-permute-done | bytes 24608 | tf_op jit(solution)/shard_map/ppermute | solution.py:22
  178.9 1.9 %collective-permute-start.13 = (f32[3,1,2048]{2,1,0:T(1,128)S(1)}, f32[3,1,2048]{2,1,0:T(1,128)S(1)}, u32[]{:S(2)}, u32[]{:S(2)}) collective-permute-start(f32[3,1,2048]{2,1,0:T(1,128)S(1)} %get-tuple-element.17), channel_id=1, source_target_pairs={{1,0},{2,1},{3,2},{4,3},{5,4},{6,5},{7,6},{8,7},{9,8},{10,9},{11,1... | collective-permute-start | bytes 73736 | tf_op jit(solution)/shard_map/ppermute | solution.py:23
  180.8 4.8 %collective-permute-start.14 = (f32[3,1,2048]{2,1,0:T(1,128)S(1)}, f32[3,1,2048]{2,1,0:T(1,128)S(1)}, u32[]{:S(2)}, u32[]{:S(2)}) collective-permute-start(f32[3,1,2048]{2,1,0:T(1,128)S(1)} %get-tuple-element.18), channel_id=1, source_target_pairs={{0,1},{1,2},{2,3},{3,4},{4,5},{5,6},{6,7},{7,8},{8,9},{9,10},{10,1... | collective-permute-start | bytes 73736 | tf_op jit(solution)/shard_map/ppermute | solution.py:22
  185.7 5.0 %collective-permute-done.14 = f32[3,1,2048]{2,1,0:T(1,128)S(1)} collective-permute-done((f32[3,1,2048]{2,1,0:T(1,128)S(1)}, f32[3,1,2048]{2,1,0:T(1,128)S(1)}, u32[]{:S(2)}, u32[]{:S(2)}) %collective-permute-start.14) | collective-permute-done | bytes 24608 | tf_op jit(solution)/shard_map/ppermute | solution.py:22
  190.7 1.3 fusion.7
  (71 shorter events, 13.5 us)
Async XLA Ops:
  0.0 128.7 %copy-start = (f32[16,16]{1,0:T(8,128)S(1)}, f32[16,16]{1,0:T(8,128)}, u32[]{:S(2)}) copy-start(f32[16,16]{1,0:T(8,128)} %param.9) | copy-start | bytes 3076
  0.0 19.7 %copy-start.1 = (f32[1,3,32,2048]{3,2,1,0:T(8,128)S(1)}, f32[1,3,32,2048]{3,2,1,0:T(8,128)}, u32[]{:S(2)}) copy-start(f32[1,3,32,2048]{3,2,1,0:T(8,128)} %param.5) | copy-start | bytes 2359300
  1.1 18.5 %collective-permute-start = (f32[3,2,2048]{2,1,0:T(2,128)S(1)}, f32[3,2,2048]{2,1,0:T(2,128)S(1)}, u32[]{:S(2)}, u32[]{:S(2)}) collective-permute-start(f32[3,2,2048]{2,1,0:T(2,128)S(1)} %get-tuple-element.35), channel_id=1, source_target_pairs={{0,1},{1,2},{2,3},{3,4},{4,5},{5,6},{6,7},{7,8},{8,9},{9,10},{10,1... | collective-permute-start | bytes 147464 | tf_op jit(solution)/shard_map/ppermute | solution.py:22
  5.6 14.0 %collective-permute-start.1 = (f32[3,2,2048]{2,1,0:T(2,128)S(1)}, f32[3,2,2048]{2,1,0:T(2,128)S(1)}, u32[]{:S(2)}, u32[]{:S(2)}) collective-permute-start(f32[3,2,2048]{2,1,0:T(2,128)S(1)} %get-tuple-element.36), channel_id=1, source_target_pairs={{1,0},{2,1},{3,2},{4,3},{5,4},{6,5},{7,6},{8,7},{9,8},{10,9},{11,1... | collective-permute-start | bytes 147464 | tf_op jit(solution)/shard_map/ppermute | solution.py:23
  12.8 8.5 %collective-permute-start.3 = (f32[2,6,2048]{2,0,1:T(2,128)S(1)}, f32[2,6,2048]{2,0,1:T(2,128)S(1)}, u32[]{:S(2)}, u32[]{:S(2)}) collective-permute-start(f32[2,6,2048]{2,0,1:T(2,128)S(1)} %copy.66), channel_id=1, source_target_pairs={{1,0},{2,1},{3,2},{4,3},{5,4},{6,5},{7,6},{8,7},{9,8},{10,9},{11,1... | collective-permute-start | bytes 294920 | tf_op jit(solution)/shard_map/ppermute | solution.py:23
  14.8 11.1 %collective-permute-start.2 = (f32[2,6,2048]{2,0,1:T(2,128)S(1)}, f32[2,6,2048]{2,0,1:T(2,128)S(1)}, u32[]{:S(2)}, u32[]{:S(2)}) collective-permute-start(f32[2,6,2048]{2,0,1:T(2,128)S(1)} %copy.65), channel_id=1, source_target_pairs={{0,1},{1,2},{2,3},{3,4},{4,5},{5,6},{6,7},{7,8},{8,9},{9,10},{10,1... | collective-permute-start | bytes 294920 | tf_op jit(solution)/shard_map/ppermute | solution.py:22
  27.2 10.2 %collective-permute-start.4 = (f32[3,2,2048]{2,1,0:T(2,128)S(1)}, f32[3,2,2048]{2,1,0:T(2,128)S(1)}, u32[]{:S(2)}, u32[]{:S(2)}) collective-permute-start(f32[3,2,2048]{2,1,0:T(2,128)S(1)} %get-tuple-element.33), channel_id=1, source_target_pairs={{0,1},{1,2},{2,3},{3,4},{4,5},{5,6},{6,7},{7,8},{8,9},{9,10},{10,1... | collective-permute-start | bytes 147464 | tf_op jit(solution)/shard_map/ppermute | solution.py:22
  29.2 10.2 %collective-permute-start.5 = (f32[3,2,2048]{2,1,0:T(2,128)S(1)}, f32[3,2,2048]{2,1,0:T(2,128)S(1)}, u32[]{:S(2)}, u32[]{:S(2)}) collective-permute-start(f32[3,2,2048]{2,1,0:T(2,128)S(1)} %get-tuple-element.34), channel_id=1, source_target_pairs={{1,0},{2,1},{3,2},{4,3},{5,4},{6,5},{7,6},{8,7},{9,8},{10,9},{11,1... | collective-permute-start | bytes 147464 | tf_op jit(solution)/shard_map/ppermute | solution.py:23
  40.7 11.1 %collective-permute-start.6 = (f32[3,2,2048]{2,1,0:T(2,128)S(1)}, f32[3,2,2048]{2,1,0:T(2,128)S(1)}, u32[]{:S(2)}, u32[]{:S(2)}) collective-permute-start(f32[3,2,2048]{2,1,0:T(2,128)S(1)} %get-tuple-element.31), channel_id=1, source_target_pairs={{0,1},{1,2},{2,3},{3,4},{4,5},{5,6},{6,7},{7,8},{8,9},{9,10},{10,1... | collective-permute-start | bytes 147464 | tf_op jit(solution)/shard_map/ppermute | solution.py:22
  43.9 9.1 %collective-permute-start.7 = (f32[3,2,2048]{2,1,0:T(2,128)S(1)}, f32[3,2,2048]{2,1,0:T(2,128)S(1)}, u32[]{:S(2)}, u32[]{:S(2)}) collective-permute-start(f32[3,2,2048]{2,1,0:T(2,128)S(1)} %get-tuple-element.32), channel_id=1, source_target_pairs={{1,0},{2,1},{3,2},{4,3},{5,4},{6,5},{7,6},{8,7},{9,8},{10,9},{11,1... | collective-permute-start | bytes 147464 | tf_op jit(solution)/shard_map/ppermute | solution.py:23
  54.1 3.2 %collective-permute-start.8 = (f32[3,32,2048]{2,1,0:T(8,128)S(1)}, f32[3,32,2048]{2,1,0:T(8,128)S(1)}, u32[]{:S(2)}, u32[]{:S(2)}) collective-permute-start(f32[3,32,2048]{2,1,0:T(8,128)S(1)} %maximum_multiply_fusion.2), channel_id=1, source_target_pairs={{0,32},{32,64},{64,96},{96,128},{128,160},{160,192},{192,224},{224... | collective-permute-start | bytes 2359304 | tf_op jit(solution)/shard_map/ppermute | solution.py:31
  147.0 10.5 %collective-permute-start.9 = (f32[3,1,2048]{2,1,0:T(1,128)S(1)}, f32[3,1,2048]{2,1,0:T(1,128)S(1)}, u32[]{:S(2)}, u32[]{:S(2)}) collective-permute-start(f32[3,1,2048]{2,1,0:T(1,128)S(1)} %get-tuple-element.29), channel_id=1, source_target_pairs={{1,0},{2,1},{3,2},{4,3},{5,4},{6,5},{7,6},{8,7},{9,8},{10,9},{11,1... | collective-permute-start | bytes 73736 | tf_op jit(solution)/shard_map/ppermute | solution.py:23
  155.5 9.9 %collective-permute-start.10 = (f32[3,1,2048]{2,1,0:T(1,128)S(1)}, f32[3,1,2048]{2,1,0:T(1,128)S(1)}, u32[]{:S(2)}, u32[]{:S(2)}) collective-permute-start(f32[3,1,2048]{2,1,0:T(1,128)S(1)} %get-tuple-element.30), channel_id=1, source_target_pairs={{0,1},{1,2},{2,3},{3,4},{4,5},{5,6},{6,7},{7,8},{8,9},{9,10},{10,1... | collective-permute-start | bytes 73736 | tf_op jit(solution)/shard_map/ppermute | solution.py:22
  166.2 6.9 %collective-permute-start.11 = (f32[3,1,2048]{2,1,0:T(1,128)S(1)}, f32[3,1,2048]{2,1,0:T(1,128)S(1)}, u32[]{:S(2)}, u32[]{:S(2)}) collective-permute-start(f32[3,1,2048]{2,1,0:T(1,128)S(1)} %get-tuple-element.23), channel_id=1, source_target_pairs={{1,0},{2,1},{3,2},{4,3},{5,4},{6,5},{7,6},{8,7},{9,8},{10,9},{11,1... | collective-permute-start | bytes 73736 | tf_op jit(solution)/shard_map/ppermute | solution.py:23
  168.1 9.9 %collective-permute-start.12 = (f32[3,1,2048]{2,1,0:T(1,128)S(1)}, f32[3,1,2048]{2,1,0:T(1,128)S(1)}, u32[]{:S(2)}, u32[]{:S(2)}) collective-permute-start(f32[3,1,2048]{2,1,0:T(1,128)S(1)} %get-tuple-element.24), channel_id=1, source_target_pairs={{0,1},{1,2},{2,3},{3,4},{4,5},{5,6},{6,7},{7,8},{8,9},{9,10},{10,1... | collective-permute-start | bytes 73736 | tf_op jit(solution)/shard_map/ppermute | solution.py:22
  178.9 6.9 %collective-permute-start.13 = (f32[3,1,2048]{2,1,0:T(1,128)S(1)}, f32[3,1,2048]{2,1,0:T(1,128)S(1)}, u32[]{:S(2)}, u32[]{:S(2)}) collective-permute-start(f32[3,1,2048]{2,1,0:T(1,128)S(1)} %get-tuple-element.17), channel_id=1, source_target_pairs={{1,0},{2,1},{3,2},{4,3},{5,4},{6,5},{7,6},{8,7},{9,8},{10,9},{11,1... | collective-permute-start | bytes 73736 | tf_op jit(solution)/shard_map/ppermute | solution.py:23
  180.8 9.9 %collective-permute-start.14 = (f32[3,1,2048]{2,1,0:T(1,128)S(1)}, f32[3,1,2048]{2,1,0:T(1,128)S(1)}, u32[]{:S(2)}, u32[]{:S(2)}) collective-permute-start(f32[3,1,2048]{2,1,0:T(1,128)S(1)} %get-tuple-element.18), channel_id=1, source_target_pairs={{0,1},{1,2},{2,3},{3,4},{4,5},{5,6},{6,7},{7,8},{8,9},{9,10},{10,1... | collective-permute-start | bytes 73736 | tf_op jit(solution)/shard_map/ppermute | solution.py:22
where the time goes:
time: 193 us; the launch traced here: 192 us
  starting transfers between devices  62.6 us (32%)
  blocking collectives  45.7 us (24%)
  local copies, waits for them, and re-layouts  30.3 us (16%)
  waiting for transfers between devices  29.8 us (15%)
  other arithmetic  22.5 us (12%)
    ppermute x7, starting transfers between devices, with_halo(): after = lax.ppermute(first, axis, down)  35.2 us
    all_to_all x1, blocking collectives, local(): lax.all_to_all(jumps[None], 'sub', split_axis=3, concat_axis=0, tiled=True)  29.4 us
    ppermute x7, starting transfers between devices, with_halo(): before = lax.ppermute(last, axis, up)  26 us
    ppermute x7, waiting for transfers between devices, with_halo(): before = lax.ppermute(last, axis, up)  23.1 us
    all_to_all x1, blocking collectives, local(): lax.all_to_all(mixed_parts, 'sub', split_axis=0, concat_axis=3, tiled=True)  16.3 us
    unnamed x10, local copies, waits for them, and re-layouts  12.8 us
    unnamed x1, other arithmetic  11.9 us
    broadcast_in_dim x1, local copies, waits for them, and re-layouts, local(): jumps[None]  6.94 us
  transfers between devices with their start and end apart: 15, of which 10 were waited for; matrix products, arithmetic and copies ran while one was open for 1% of the time, Pallas kernels for 0%

commit v1 on v0

v1 whole, which is shorter than its diff:
```python
import jax
import jax.numpy as jnp
from jax import lax
from jax.experimental import pallas as pl
from jax.experimental.pallas import tpu as pltpu
from jax.sharding import PartitionSpec as P

FSTEPS = 3
DSTEPS = 3
S = 16
F = 3
G = 4
L = 128
R = 9
W = 2 * R
NMAIN = F * G

VMEM = pl.BlockSpec(memory_space=pltpu.VMEM)
SMEM = pl.BlockSpec(memory_space=pltpu.SMEM)
F32 = jnp.float32


def iota(dim, shape=(8, L)):
    return lax.broadcasted_iota(jnp.int32, shape, dim)


def lookup(classes, table):
    value = jnp.full(classes.shape, table[0], F32)
    for i in range(1, table.shape[0]):
        value = jnp.where(classes == i, table[i], value)
    return value


def pack_kernel(x_ref, o_ref):
    lane = iota(1)

    def tile(f, g, c):
        return x_ref[f, 8 * g : 8 * g + 8, L * (c % S) : L * (c % S) + L]

    for c in range(S):
        for f in range(F):
            for g in range(G):
                o_ref[c, f * G + g] = tile(f, g, c)
        for j in range(2):
            packed = jnp.zeros((8, L), F32)
            for q in range(6):
                f, g = q % 3, 2 * j + q // 3
                sides = jnp.where(lane < 64, tile(f, g, c + 1), tile(f, g, c - 1))
                sides = pltpu.roll(sides, W * q + R, 1)
                packed = jnp.where((lane >= W * q) & (lane < W * q + W), sides, packed)
            o_ref[c, NMAIN + j] = packed


def terrain_tiles(ter_ref, chunk, g):
    def tile(c):
        start = pl.multiple_of(lax.rem(c + S, S) * L, L)
        return ter_ref[8 * g : 8 * g + 8, pl.ds(start, L)]

    return tile(chunk), jnp.where(iota(1) < 64, tile(chunk + 1), tile(chunk - 1))


def edge_kernel(chunk_ref, depth_ref, x_ref, ter_ref, up_ref, down_ref):
    lane, row = iota(1), iota(0)
    chunk = chunk_ref[0]

    def depth_of(g, q):
        own, sides = terrain_tiles(ter_ref, chunk, g)
        return lookup(own, depth_ref), pltpu.roll(lookup(sides, depth_ref), W * q + R, 1)

    def send(o_ref, g, inner, edge, turn, sign, halo, flux_at, height_at, even_by, odd_by):
        depth_own, depth_sides = depth_of(inner, flux_at)
        own, sides = terrain_tiles(ter_ref, chunk, g)
        o_ref[56] = own.astype(F32)
        sides = pltpu.roll(sides.astype(F32), 108 + R, 1)
        at_edge = row == edge
        at_height = at_edge & (lane >= W * height_at) & (lane < W * height_at + W)
        by = (W * (height_at - flux_at)) % L
        packed = []
        for t in range(S):
            flux = pltpu.roll(depth_own * x_ref[t, G + inner], turn, 0)
            o_ref[t * F] = x_ref[t, g] + jnp.where(at_edge, sign * flux, 0.0)
            o_ref[t * F + 1] = x_ref[t, G + g]
            o_ref[t * F + 2] = x_ref[t, 2 * G + g]
            columns = x_ref[t, NMAIN + halo]
            flux = pltpu.roll(pltpu.roll(depth_sides * columns, by, 1), turn, 0)
            columns = columns + jnp.where(at_height, sign * flux, 0.0)
            shift = odd_by if t % 2 else even_by
            packed.append(pltpu.roll(columns, shift, 1) if shift else columns)
        for j in range(S // 2):
            o_ref[48 + j] = jnp.where(
                lane < 54, packed[2 * j], jnp.where(lane < 108, packed[2 * j + 1], sides)
            )

    send(up_ref, 0, 1, 7, 7, -0.25, 0, 4, 0, 0, 54)
    send(down_ref, 3, 2, 0, 1, 0.25, 1, 1, 3, L - 54, 0)


def main_kernel(
    place_ref, depth_ref, spread_ref, mix_ref, x_ref, ter_ref, above_ref, below_ref,
    o_ref, depth_s, kappa_s, ends_s, jumps_s,
):
    rows, cols = 8 * (G + 2), 2 * L
    chunk, first, total = place_ref[0], place_ref[1], place_ref[2]
    row = iota(0, (rows, cols))
    index = row + (first - 8)
    inside = ((index >= 0) & (index < total)).astype(F32)
    slope = -0.25 * inside

    def back(value, by):
        return pltpu.roll(value, (L - by) % L, 1)

    def grid(tiles):
        return jnp.concatenate([jnp.concatenate(pair, axis=1) for pair in tiles], axis=0)

    def terrain_halo(ref):
        return ref[56].astype(jnp.int32), back(ref[48], 108 + R).astype(jnp.int32)

    classes = grid(
        [terrain_halo(above_ref)]
        + [terrain_tiles(ter_ref, chunk, g) for g in range(G)]
        + [terrain_halo(below_ref)]
    )
    depth_s[...] = lookup(classes, depth_ref)
    kappa_s[...] = lookup(classes, spread_ref) * inside
    ends_s[...] = jnp.zeros(ends_s.shape, F32)

    def before(value, dim):
        return pltpu.roll(value, 1, dim)

    def after(value, dim):
        return pltpu.roll(value, value.shape[dim] - 1, dim)

    def model(h, u, v, outer):
        depth = depth_s[...]
        flux_x, flux_y = depth * u, depth * v
        up, down = before(flux_x, 0), after(flux_x, 0)
        if outer:
            up = jnp.where(row == 0, 0.0, up)
            down = jnp.where(row == rows - 1, 0.0, down)
        h = h + slope * ((down - up) + (after(flux_y, 1) - before(flux_y, 1)))
        new_u = u + slope * (after(h, 0) - before(h, 0)) + 0.15 * v
        new_v = v - 0.25 * (after(h, 1) - before(h, 1)) - 0.15 * u
        return h, new_u, new_v

    def spread(w):
        kappa = kappa_s[...]
        around = (after(w, 0) + before(w, 0)) + (after(w, 1) + before(w, 1))
        return (1.0 - 4.0 * kappa) * w + kappa * around

    def one(t, half, pair):
        state = []
        for f in range(F):
            by = W * f + 54 * half + R
            tiles = [(above_ref[t * F + f], back(above_ref[48 + pair], by))]
            for g in range(G):
                q = (g % 2) * 3 + f
                tiles.append((x_ref[t, f * G + g], back(x_ref[t, NMAIN + g // 2], W * q + R)))
            tiles.append((below_ref[t * F + f], back(below_ref[48 + pair], by)))
            state.append(grid(tiles))
        jumps = [state[f] - ends_s[f] for f in range(F)]
        for step in range(FSTEPS):
            state = model(*state, step == 0)
        for f in range(F):
            ends_s[f] = state[f]
        for f in range(F):
            w = jumps[f]
            for step in range(DSTEPS):
                w = spread(w)
            for g in range(G):
                jumps_s[t, f * G + g] = w[8 + 8 * g : 16 + 8 * g, :L]

    def two(pair, carry):
        one(2 * pair, 0, pair)
        one(2 * pair + 1, 1, pair)
        return carry

    lax.fori_loop(0, S // 2, two, 0)

    def mix(part, carry):
        base = part * 3
        held = [[jumps_s[t, base + i] for i in range(3)] for t in range(S)]
        for s in range(S):
            sums = [mix_ref[s, 0] * held[0][i] for i in range(3)]
            for t in range(1, S):
                weight = mix_ref[s, t]
                sums = [sums[i] + weight * held[t][i] for i in range(3)]
            for i in range(3):
                o_ref[s, base + i] = sums[i]
        return carry

    lax.fori_loop(0, NMAIN // 3, mix, 0)


def local(states, terrain, depth_table, spread_table, mixing):
    strips = lax.axis_size("tile")
    rows = states.shape[2]
    chunk = lax.axis_index("sub").astype(jnp.int32)
    first = lax.axis_index("tile").astype(jnp.int32) * rows
    place = jnp.stack([chunk, first, jnp.int32(rows * strips)])

    chunks = pl.pallas_call(
        pack_kernel,
        out_shape=jax.ShapeDtypeStruct((S, NMAIN + 2, 8, L), F32),
        in_specs=[VMEM],
        out_specs=VMEM,
    )(states[0])
    held = lax.all_to_all(chunks, "sub", split_axis=0, concat_axis=0, tiled=True)
    halo = jax.ShapeDtypeStruct((57, 8, L), F32)
    up, down = pl.pallas_call(
        edge_kernel,
        out_shape=(halo, halo),
        in_specs=[SMEM, SMEM, VMEM, VMEM],
        out_specs=(VMEM, VMEM),
    )(place, depth_table, held, terrain)
    forth = [(i, i + 1) for i in range(strips - 1)]
    above = lax.ppermute(down, "tile", forth)
    below = lax.ppermute(up, "tile", [(j, i) for i, j in forth])
    wide = (8 * (G + 2), 2 * L)
    mixed = pl.pallas_call(
        main_kernel,
        out_shape=jax.ShapeDtypeStruct((S, NMAIN, 8, L), F32),
        in_specs=[SMEM, SMEM, SMEM, SMEM, VMEM, VMEM, VMEM, VMEM],
        out_specs=VMEM,
        scratch_shapes=[
            pltpu.VMEM(wide, F32),
            pltpu.VMEM(wide, F32),
            pltpu.VMEM((F,) + wide, F32),
            pltpu.VMEM((S, NMAIN, 8, L), F32),
        ],
    )(place, depth_table, spread_table, mixing, held, terrain, above, below)
    parts = lax.all_to_all(mixed, "sub", split_axis=0, concat_axis=0, tiled=True)
    parts = parts.reshape(S, F, rows, L).transpose(1, 2, 0, 3)
    return parts.reshape(1, F, rows, S * L)


def solution(mesh):
    in_specs = (P("sub", None, "tile", None), P("tile", None), P(), P(), P())
    out_specs = P("sub", None, "tile", None)
    return jax.shard_map(local, mesh=mesh, in_specs=in_specs, out_specs=out_specs, check_vma=False)
```

time: 193 us -> 85.9 us (0.45)
  the two profiles are of different devices: /device:TPU:256 before, /device:TPU:249 now
where the time goes in v1:
time: 85.9 us; the launch traced here: 85.5 us
  blocking collectives  23.4 us (27%)
  waiting for transfers between devices  23.2 us (27%)
  Pallas kernels  21.7 us (25%)
  starting transfers between devices  13.4 us (16%)
  local copies, waits for them, and re-layouts  3.11 us (4%)
    all_to_all x1, blocking collectives, local(): lax.all_to_all(mixed, 'sub', split_axis=0, concat_axis=0, tiled=True)  23.4 us
    pallas_call x1, Pallas kernels, local(): pl.pallas_call(main_kernel, out_shape=jax.ShapeDtypeStruct((S, NMAIN, 8,...  17.1 us
    all_to_all x1, waiting for transfers between devices, local(): lax.all_to_all(chunks, 'sub', split_axis=0, concat_axis=0, tiled=True)  12.7 us
    ppermute x1, waiting for transfers between devices, local(): above = lax.ppermute(down, 'tile', forth)  7.31 us
    all_to_all x1, starting transfers between devices, local(): lax.all_to_all(chunks, 'sub', split_axis=0, concat_axis=0, tiled=True)  6.09 us
    ppermute x1, starting transfers between devices, local(): above = lax.ppermute(down, 'tile', forth)  5.42 us
    ppermute x1, waiting for transfers between devices, local(): below = lax.ppermute(up, 'tile', [(j, i) for i, j in forth])  3.22 us
    pallas_call x1, Pallas kernels, local(): pl.pallas_call(pack_kernel, out_shape=jax.ShapeDtypeStruct((S, NMAIN + 2,...  2.35 us
  transfers between devices with their start and end apart: 3, of which 3 were waited for; matrix products, arithmetic and copies ran while one was open for 1% of the time, Pallas kernels for 0%

profile of v1, /device:TPU:249, one launch (start us, length us, event | category | flops | bytes accessed | tf_op | source)
XLA Modules:
  0.0 85.5 jit_solution(18285635551956621851)
XLA Ops:
  0.0 2.4 %shard_map.55 = f32[16,14,8,128]{3,2,1,0:T(8,128)} custom-call(f32[3,32,2048]{2,1,0:T(8,128)} %bitcast.9), custom_call_target="tpu_custom_call" | custom-call | tf_op jit(solution)/shard_map/pallas_call | solution.py:201
  2.4 6.1 %all-to-all-start = ((f32[16,14,8,128]{3,2,1,0:T(8,128)}), f32[16,14,8,128]{3,2,1,0:T(8,128)S(1)}, u32[]{:S(2)}, u32[]{:S(2)}) async-start(f32[16,14,8,128]{3,2,1,0:T(8,128)} %shard_map.55), calls=%async_computation | async-start | bytes 1835008 | tf_op jit(solution)/shard_map/all_to_all | solution.py:207
  8.4 0.6 pad_add_fusion.chunk_ref.place_ref
  9.0 12.7 %all-to-all-done.x_ref = f32[16,14,8,128]{3,2,1,0:T(8,128)S(1)} async-done(((f32[16,14,8,128]{3,2,1,0:T(8,128)}), f32[16,14,8,128]{3,2,1,0:T(8,128)S(1)}, u32[]{:S(2)}, u32[]{:S(2)}) %all-to-all-start) | async-done | bytes 917536 | tf_op jit(solution)/shard_map/all_to_all | solution.py:207
  21.7 0.0 copy-start
  21.7 0.9 %copy-done = f32[16,14,8,128]{3,2,1,0:T(8,128)} copy-done((f32[16,14,8,128]{3,2,1,0:T(8,128)}, f32[16,14,8,128]{3,2,1,0:T(8,128)S(1)}, u32[]{:S(2)}) %copy-start) | copy-done | bytes 917528
  22.7 2.3 %shard_map.56 = (f32[57,8,128]{2,1,0:T(8,128)}, f32[57,8,128]{2,1,0:T(8,128)}) custom-call(s32[3]{0:T(128)} %pad_add_fusion.chunk_ref.place_ref, f32[8]{0:T(128)} %depth_ref.3, f32[16,14,8,128]{3,2,1,0:T(8,128)} %copy-done, s32[32,2048]{1,0:T(8,128)} %ter_ref.3), custom_call_target="tpu_custom_call" | custom-call | tf_op jit(solution)/shard_map/pallas_call | solution.py:209
  24.9 5.4 %collective-permute-start = (f32[57,8,128]{2,1,0:T(8,128)}, f32[57,8,128]{2,1,0:T(8,128)S(1)}, u32[]{:S(2)}, u32[]{:S(2)}) collective-permute-start(f32[57,8,128]{2,1,0:T(8,128)} %get-tuple-element.7), channel_id=1, source_target_pairs={{0,1},{1,2},{2,3},{3,4},{4,5},{5,6},{6,7},{7,8},{8,9},{9,10},{10,1... | collective-permute-start | bytes 700424 | tf_op jit(solution)/shard_map/ppermute | solution.py:216
  30.4 1.9 %collective-permute-start.1 = (f32[57,8,128]{2,1,0:T(8,128)}, f32[57,8,128]{2,1,0:T(8,128)S(1)}, u32[]{:S(2)}, u32[]{:S(2)}) collective-permute-start(f32[57,8,128]{2,1,0:T(8,128)} %get-tuple-element.8), channel_id=1, source_target_pairs={{1,0},{2,1},{3,2},{4,3},{5,4},{6,5},{7,6},{8,7},{9,8},{10,9},{11,1... | collective-permute-start | bytes 700424 | tf_op jit(solution)/shard_map/ppermute | solution.py:217
  32.3 7.3 %collective-permute-done.above_ref = f32[57,8,128]{2,1,0:T(8,128)S(1)} collective-permute-done((f32[57,8,128]{2,1,0:T(8,128)}, f32[57,8,128]{2,1,0:T(8,128)S(1)}, u32[]{:S(2)}, u32[]{:S(2)}) %collective-permute-start) | collective-permute-done | bytes 233504 | tf_op jit(solution)/shard_map/ppermute | solution.py:216
  39.6 0.0 copy-start.1
  39.6 3.2 %collective-permute-done.1.below_ref = f32[57,8,128]{2,1,0:T(8,128)S(1)} collective-permute-done((f32[57,8,128]{2,1,0:T(8,128)}, f32[57,8,128]{2,1,0:T(8,128)S(1)}, u32[]{:S(2)}, u32[]{:S(2)}) %collective-permute-start.1) | collective-permute-done | bytes 233504 | tf_op jit(solution)/shard_map/ppermute | solution.py:217
  42.8 0.0 copy-done.1
  42.8 0.0 copy-start.2
  42.8 0.7 copy-done.2
  43.5 17.1 %shard_map.57 = f32[16,12,8,128]{3,2,1,0:T(8,128)} custom-call(s32[3]{0:T(128)} %pad_add_fusion.chunk_ref.place_ref, f32[8]{0:T(128)} %depth_ref.3, f32[8]{0:T(128)} %spread_ref.1, f32[16,16]{1,0:T(8,128)} %mix_ref.1, f32[16,14,8,128]{3,2,1,0:T(8,128)} %copy-done, s32[32,2048]{1,0:T(8,128)} %ter_ref.3, f32[57,8,128]{2,1,0:T(8,128)} %copy-done.1, ...), custom_call_target="tpu_custom_call" | custom-call | tf_op jit(solution)/shard_map/pallas_call | solution.py:219
  60.6 23.4 %all_to_all.10 = f32[16,12,8,128]{3,2,1,0:T(8,128)S(1)} all-to-all(f32[16,12,8,128]{3,2,1,0:T(8,128)} %shard_map.57), channel_id=1, replica_groups=mesh['sub'=16,'tile'=32] {'sub'}, dimensions={0} | all-to-all | bytes 1572864 | tf_op jit(solution)/shard_map/all_to_all | solution.py:231
  84.0 0.5 copy.6
  84.5 1.0 %reshape.7 = f32[1,3,32,2048]{3,2,1,0:T(8,128)} reshape(f32[3,32,16,128]{3,2,1,0:T(8,128)S(1)} %copy.6) | data formatting | bytes 1572864 | tf_op jit(solution)/shard_map/reshape | solution.py:233
Async XLA Ops:
  2.4 19.4 %all-to-all-start = ((f32[16,14,8,128]{3,2,1,0:T(8,128)}), f32[16,14,8,128]{3,2,1,0:T(8,128)S(1)}, u32[]{:S(2)}, u32[]{:S(2)}) async-start(f32[16,14,8,128]{3,2,1,0:T(8,128)} %shard_map.55), calls=%async_computation | async-start | bytes 1835008 | tf_op jit(solution)/shard_map/all_to_all | solution.py:207
  21.7 0.9 %copy-start = (f32[16,14,8,128]{3,2,1,0:T(8,128)}, f32[16,14,8,128]{3,2,1,0:T(8,128)S(1)}, u32[]{:S(2)}) copy-start(f32[16,14,8,128]{3,2,1,0:T(8,128)S(1)} %all-to-all-done.x_ref) | copy-start | bytes 2752516
  24.9 14.7 %collective-permute-start = (f32[57,8,128]{2,1,0:T(8,128)}, f32[57,8,128]{2,1,0:T(8,128)S(1)}, u32[]{:S(2)}, u32[]{:S(2)}) collective-permute-start(f32[57,8,128]{2,1,0:T(8,128)} %get-tuple-element.7), channel_id=1, source_target_pairs={{0,1},{1,2},{2,3},{3,4},{4,5},{5,6},{6,7},{7,8},{8,9},{9,10},{10,1... | collective-permute-start | bytes 700424 | tf_op jit(solution)/shard_map/ppermute | solution.py:216
  30.4 12.5 %collective-permute-start.1 = (f32[57,8,128]{2,1,0:T(8,128)}, f32[57,8,128]{2,1,0:T(8,128)S(1)}, u32[]{:S(2)}, u32[]{:S(2)}) collective-permute-start(f32[57,8,128]{2,1,0:T(8,128)} %get-tuple-element.8), channel_id=1, source_target_pairs={{1,0},{2,1},{3,2},{4,3},{5,4},{6,5},{7,6},{8,7},{9,8},{10,9},{11,1... | collective-permute-start | bytes 700424 | tf_op jit(solution)/shard_map/ppermute | solution.py:217
  39.6 3.2 %copy-start.1 = (f32[57,8,128]{2,1,0:T(8,128)}, f32[57,8,128]{2,1,0:T(8,128)S(1)}, u32[]{:S(2)}) copy-start(f32[57,8,128]{2,1,0:T(8,128)S(1)} %collective-permute-done.above_ref) | copy-start | bytes 700420
  42.8 0.7 copy-start.2

commit v2 on v1

v2 whole, which is shorter than its diff:
```python
import jax
import jax.numpy as jnp
from jax import lax
from jax.experimental import pallas as pl
from jax.experimental.pallas import tpu as pltpu
from jax.sharding import PartitionSpec as P

FSTEPS = 3
DSTEPS = 3
S = 16
F = 3
G = 4
L = 128
R = 8
C = 9
W = 2 * C
NMAIN = F * G
NALL = NMAIN + 2
NHALO = S * F + S // 2
BLOCKS = 8
DEPTH = 6
EDGE = 16
TALL = L + 2 * EDGE
PART = 16

VMEM = pl.BlockSpec(memory_space=pltpu.VMEM)
SMEM = pl.BlockSpec(memory_space=pltpu.SMEM)
F32 = jnp.float32


def iota(dim, shape=(8, L)):
    return lax.broadcasted_iota(jnp.int32, shape, dim)


def lookup(classes, table):
    value = jnp.full(classes.shape, table[0], F32)
    for i in range(1, table.shape[0]):
        value = jnp.where(classes == i, table[i], value)
    return value


def pack_kernel(x_ref, o_ref):
    lane = iota(1)

    def tile(f, g, c):
        return x_ref[f, 8 * g : 8 * g + 8, L * (c % S) : L * (c % S) + L]

    for c in range(S):
        for f in range(F):
            for g in range(G):
                o_ref[c, f * G + g] = tile(f, g, c)
        for j in range(2):
            packed = jnp.zeros((8, L), F32)
            for q in range(6):
                f, g = q % 3, 2 * j + q // 3
                sides = jnp.where(lane < 64, tile(f, g, c + 1), tile(f, g, c - 1))
                sides = pltpu.roll(sides, W * q + C, 1)
                packed = jnp.where((lane >= W * q) & (lane < W * q + W), sides, packed)
            o_ref[c, NMAIN + j] = packed


def terrain_tiles(ter_ref, chunk, g):
    def tile(c):
        start = pl.multiple_of(lax.rem(c + S, S) * L, L)
        return ter_ref[8 * g : 8 * g + 8, pl.ds(start, L)]

    return tile(chunk), jnp.where(iota(1) < 64, tile(chunk + 1), tile(chunk - 1))


def edge_kernel(place_ref, depth_ref, x_ref, ter_ref, up_ref, down_ref):
    lane, row = iota(1), iota(0)
    chunk = place_ref[0]

    def send(o_ref, g, inner, edge, turn, sign, halo, flux_at, height_at, low_by, high_by):
        own, sides = terrain_tiles(ter_ref, chunk, inner)
        depth_own = sign * lookup(own, depth_ref)
        depth_sides = pltpu.roll(sign * lookup(sides, depth_ref), W * flux_at + C, 1)
        at_edge = row == edge
        at_height = at_edge & (lane >= W * height_at) & (lane < W * height_at + W)
        by = (W * (height_at - flux_at)) % L
        packed = []
        for t in range(S):
            flux = pltpu.roll(depth_own * x_ref[t, G + inner], turn, 0)
            o_ref[t * F] = x_ref[t, g] + jnp.where(at_edge, flux, 0.0)
            o_ref[t * F + 1] = x_ref[t, G + g]
            o_ref[t * F + 2] = x_ref[t, 2 * G + g]
            columns = x_ref[t, NMAIN + halo]
            flux = pltpu.roll(pltpu.roll(depth_sides * columns, by, 1), turn, 0)
            columns = columns + jnp.where(at_height, flux, 0.0)
            shift = low_by if t < S // 2 else high_by
            packed.append(pltpu.roll(columns, shift, 1) if shift else columns)
        for j in range(S // 2):
            o_ref[S * F + j] = jnp.where(lane < 3 * W, packed[j], packed[j + S // 2])

    send(up_ref, 0, 1, 7, 7, -0.25, 0, 4, 0, 0, 3 * W)
    send(down_ref, 3, 2, 0, 1, 0.25, 1, 1, 3, L - 3 * W, 0)


def terrain_kernel(place_ref, ter_ref, up_ref, down_ref):
    up_ref[0], up_ref[1] = terrain_tiles(ter_ref, place_ref[0], 0)
    down_ref[0], down_ref[1] = terrain_tiles(ter_ref, place_ref[0], G - 1)


def row_of(block, r):
    return DEPTH * block + r - R


def inside_of(first, total, r, shape):
    index = DEPTH * lax.div(iota(1, shape), S) + (r - R) + first
    return ((index >= 0) & (index < total)).astype(F32)


def coef_kernel(place_ref, depth_ref, spread_ref, ter_ref, above_ref, below_ref, o_ref, table_s):
    chunk, first, total = place_ref[0], place_ref[1], place_ref[2]
    lane = iota(1)
    tiles = [(above_ref[0], above_ref[1])]
    tiles += [terrain_tiles(ter_ref, chunk, g) for g in range(G)]
    tiles += [(below_ref[0], below_ref[1])]
    for i, (own, sides) in enumerate(tiles):
        rows = slice(8 * i, 8 * i + 8)
        table_s[0, rows] = lookup(own, depth_ref)
        table_s[1, rows] = lookup(own, spread_ref)
        depth = pltpu.roll(lookup(sides, depth_ref), C, 1)
        spread = pltpu.roll(lookup(sides, spread_ref), W + C, 1)
        table_s[2, rows] = jnp.where(lane < W, depth, spread)
    for r in range(DEPTH):
        inside = inside_of(first, total, r, (1, L))

        def turned(k):
            rows = [
                jnp.broadcast_to(table_s[k, pl.ds(row_of(b, r) + R, 1), :], (S, L))
                for b in range(BLOCKS)
            ]
            return jnp.concatenate(rows, axis=0).T

        sides = turned(2)
        for k in range(2):
            scale = inside if k else 1.0
            o_ref[k, r, 0:8, :] = jnp.zeros((8, L), F32)
            o_ref[k, r, TALL - 8 :, :] = jnp.zeros((8, L), F32)
            o_ref[k, r, EDGE : EDGE + L, :] = turned(k) * scale
            o_ref[k, r, EDGE - C : EDGE, :] = sides[W * k : W * k + C] * scale
            o_ref[k, r, EDGE + L : EDGE + L + C, :] = sides[W * k + C : W * k + W] * scale


def main_kernel(
    place_ref, x_ref, above_ref, below_ref, coef_ref, weights_ref, o_ref,
    a_s, b_s, flux_s, slope_s,
):
    first, total = place_ref[1], place_ref[2]
    lane = iota(1, (PART, L))

    for buffer in (a_s, b_s):
        for f in range(F):
            for r in range(DEPTH):
                buffer[f, r, 0:8, :] = jnp.zeros((8, L), F32)
                buffer[f, r, TALL - 8 :, :] = jnp.zeros((8, L), F32)
    for r in range(DEPTH):
        slope_s[r] = -0.25 * inside_of(first, total, r, (PART, L))

    def main_rows(f, row):
        if row < 0:
            return above_ref[pl.ds(8 * f + row + R, S, 8 * F), :]
        if row < 8 * G:
            return x_ref[pl.ds(8 * G * f + row, S, 8 * NALL), :]
        return below_ref[pl.ds(8 * f + row - 8 * G, S, 8 * F), :]

    def side_rows(row):
        if 0 <= row < 8 * G:
            g = row // 8
            value = x_ref[pl.ds(8 * (NMAIN + g // 2) + row % 8, S, 8 * NALL), :]
            return pltpu.roll(value, L - 3 * W, 1) if g % 2 else value
        ref, at = (above_ref, row + R) if row < 0 else (below_ref, row - 8 * G)
        value = ref[pl.ds(8 * S * F + at, S // 2, 8), :]
        return jnp.concatenate([value, pltpu.roll(value, L - 3 * W, 1)], axis=0)

    for r in range(DEPTH):
        for f in range(F):
            rows = [main_rows(f, row_of(b, r)) for b in range(BLOCKS)]
            a_s[f, r, EDGE : EDGE + L, :] = jnp.concatenate(rows, axis=0).T
        rows = [side_rows(row_of(b, r)) for b in range(BLOCKS)]
        sides = jnp.concatenate(rows, axis=0).T
        for f in range(F):
            a_s[f, r, EDGE - C : EDGE, :] = sides[W * f : W * f + C]
            a_s[f, r, EDGE + L : EDGE + L + C, :] = sides[W * f + C : W * f + W]

    parts = [8 + PART * i for i in range((TALL - 16) // PART)]

    def at(ref, r, start, by=0):
        return ref[r, start + by : start + by + PART, :]

    def coef(k, r, start):
        return coef_ref[k, r, start : start + PART, :]

    def neighbours(planes, r, sealed=False):
        up = planes[r - 1] if r else pltpu.roll(planes[-1], S, 1)
        down = planes[r + 1] if r < DEPTH - 1 else pltpu.roll(planes[0], L - S, 1)
        if sealed and r == 0:
            up = jnp.where(lane < S, 0.0, up)
        if sealed and r == DEPTH - 1:
            down = jnp.where(lane >= L - S, 0.0, down)
        return up, down

    def model(src, dst, step):
        h_in, u_in, v_in = src.at[0], src.at[1], src.at[2]
        h_out, u_out, v_out = dst.at[0], dst.at[1], dst.at[2]
        if step == 0:
            for r in range(DEPTH):
                flux_s[r] = coef_ref[0, r] * v_in[r]
        for p in parts:
            flux = [coef(0, r, p) * at(u_in, r, p) for r in range(DEPTH)]
            for r in range(DEPTH):
                up, down = neighbours(flux, r, step == 0)
                out = (down - up) + (at(flux_s, r, p, 1) - at(flux_s, r, p, -1))
                h_out[r, p : p + PART, :] = at(h_in, r, p) + slope_s[r] * out
        for p in parts:
            height = [at(h_out, r, p) for r in range(DEPTH)]
            for r in range(DEPTH):
                up, down = neighbours(height, r)
                u, v = at(u_in, r, p), at(v_in, r, p)
                new_v = v - 0.25 * (at(h_out, r, p, 1) - at(h_out, r, p, -1)) - 0.15 * u
                u_out[r, p : p + PART, :] = u + slope_s[r] * (down - up) + 0.15 * v
                v_out[r, p : p + PART, :] = new_v
                if step < FSTEPS - 1:
                    flux_s[r, p : p + PART, :] = coef(0, r, p) * new_v

    for step in range(FSTEPS):
        model(b_s if step else a_s, b_s, step)

    starts = lax.rem(lane, S) == 0
    for f in range(F):
        for p in parts:
            for r in range(DEPTH):
                ends = pltpu.roll(at(b_s.at[f], r, p), 1, 1)
                a_s[f, r, p : p + PART, :] = at(a_s.at[f], r, p) - jnp.where(starts, 0.0, ends)

    def spread(src, dst):
        for p in parts:
            for f in range(F):
                planes = [at(src.at[f], r, p) for r in range(DEPTH)]
                for r in range(DEPTH):
                    kappa = coef(1, r, p)
                    up, down = neighbours(planes, r)
                    around = (up + down) + (at(src.at[f], r, p, 1) + at(src.at[f], r, p, -1))
                    value = (1.0 - 4.0 * kappa) * planes[r] + kappa * around
                    dst[f, r, p : p + PART, :] = value

    buffers = [a_s, b_s]
    for step in range(DSTEPS):
        spread(buffers[step % 2], buffers[(step + 1) % 2])
    smooth = buffers[DSTEPS % 2]

    weights = weights_ref[...]
    for f in range(F):
        for r in range(DEPTH):
            mixed = lax.dot_general(
                weights,
                smooth[f, r, EDGE : EDGE + L, :],
                (((1,), (1,)), ((), ())),
                precision=lax.Precision.HIGHEST,
                preferred_element_type=F32,
            )
            for b in range(BLOCKS):
                row = row_of(b, r)
                if 0 <= row < 8 * G:
                    o_ref[pl.ds(8 * G * f + row, S, 8 * NMAIN), :] = mixed[S * b : S * b + S]


def unpack_kernel(x_ref, o_ref, sems):
    copies = [
        pltpu.make_async_copy(x_ref.at[c], o_ref.at[:, :, pl.ds(L * c, L)], sems.at[c])
        for c in range(S)
    ]
    for copy in copies:
        copy.start()
    for copy in copies:
        copy.wait()


def kernel(body, out, operands, scalars=0, scratch=(), out_specs=VMEM):
    specs = [SMEM] * scalars + [VMEM] * (len(operands) - scalars)
    return pl.pallas_call(
        body,
        out_shape=out,
        in_specs=specs,
        out_specs=(out_specs,) * len(out) if isinstance(out, tuple) else out_specs,
        scratch_shapes=list(scratch),
        compiler_params=pltpu.CompilerParams(vmem_limit_bytes=12 * 2**20),
    )(*operands)


def kept(x):
    return pltpu.with_memory_space_constraint(x, pltpu.VMEM)


def local(states, terrain, depth_table, spread_table, mixing):
    strips = lax.axis_size("tile")
    rows = states.shape[2]
    chunk = lax.axis_index("sub").astype(jnp.int32)
    first = lax.axis_index("tile").astype(jnp.int32) * rows
    place = jnp.stack([chunk, first, jnp.int32(rows * strips)])
    forth = [(i, i + 1) for i in range(strips - 1)]
    back = [(j, i) for i, j in forth]

    chunks = kernel(pack_kernel, pltpu.VMEM((S, NALL, 8, L), F32), (states[0],))
    held = lax.all_to_all(chunks, "sub", split_axis=0, concat_axis=0, tiled=True)

    edge = pltpu.VMEM((2, 8, L), jnp.int32)
    up, down = kernel(terrain_kernel, (edge, edge), (place, terrain), 1)
    terrain_above = lax.ppermute(down, "tile", forth)
    terrain_below = lax.ppermute(up, "tile", back)
    coef = kernel(
        coef_kernel,
        pltpu.VMEM((2, DEPTH, TALL, L), F32),
        (place, depth_table, spread_table, terrain, kept(terrain_above), kept(terrain_below)),
        3,
        [pltpu.VMEM((3, 8 * (G + 2), L), F32)],
    )
    weights = jnp.kron(jnp.eye(BLOCKS, dtype=F32), mixing)

    halo = pltpu.VMEM((NHALO, 8, L), F32)
    up, down = kernel(
        edge_kernel, (halo, halo), (place, depth_table, kept(held), terrain), 2
    )
    above = lax.ppermute(down, "tile", forth)
    below = lax.ppermute(up, "tile", back)

    plane = (DEPTH, TALL, L)
    mixed = kernel(
        main_kernel,
        pltpu.VMEM((S * NMAIN * 8, L), F32),
        (
            place,
            kept(held.reshape(S * NALL * 8, L)),
            kept(above.reshape(NHALO * 8, L)),
            kept(below.reshape(NHALO * 8, L)),
            kept(coef),
            kept(weights),
        ),
        1,
        [
            pltpu.VMEM((F,) + plane, F32),
            pltpu.VMEM((F,) + plane, F32),
            pltpu.VMEM(plane, F32),
            pltpu.VMEM((DEPTH, PART, L), F32),
        ],
    )
    parts = lax.all_to_all(
        mixed.reshape(S, F, rows, L), "sub", split_axis=0, concat_axis=0, tiled=True
    )
    gradient = kernel(
        unpack_kernel,
        jax.ShapeDtypeStruct((F, rows, S * L), F32),
        (kept(parts),),
        scratch=[pltpu.SemaphoreType.DMA((S,))],
        out_specs=pl.BlockSpec(memory_space=pl.ANY),
    )
    return gradient[None]


def solution(mesh):
    in_specs = (P("sub", None, "tile", None), P("tile", None), P(), P(), P())
    out_specs = P("sub", None, "tile", None)
    return jax.shard_map(local, mesh=mesh, in_specs=in_specs, out_specs=out_specs, check_vma=False)
```

time: 85.9 us -> 71 us (0.83)
  Pallas kernels: 21.7 us -> 10.7 us
  waiting for transfers between devices: 23.2 us -> 13.8 us
  starting transfers between devices: 13.4 us -> 20.9 us
  local copies, waits for them, and re-layouts: 3.11 us -> 1.77 us
    pallas_call x3 -> x6, Pallas kernels: 21.7 us -> 10.7 us  [kernel(): pl.pallas_call(body, out_shape=out, in_specs=specs, out_specs=(out_specs,...]
    ppermute x1 -> x3, starting transfers between devices: 1.92 us -> 9.27 us  [the longest x1 5.43 us: local(): terrain_above = lax.ppermute(down, 'tile', forth)]
    all_to_all x1, waiting for transfers between devices: 12.7 us -> 5.43 us  [local(): lax.all_to_all(chunks, 'sub', split_axis=0, concat_axis=0, tiled=True)]
    ppermute x1, waiting for transfers between devices: 7.31 us -> 5.18 us  [local(): above = lax.ppermute(down, 'tile', forth)]
    reshape x1 -> x0, local copies, waits for them, and re-layouts: 1 us -> none  [local(): return parts.reshape(1, F, rows, S * L)]
    ppermute x1 -> x3, waiting for transfers between devices: 3.22 us -> 3.21 us  [the longest x1 3.21 us: local(): below = lax.ppermute(up, 'tile', back)]
  transfers between devices with their start and end apart: 3 -> 5, of which waited for: 3 -> 3; matrix products, arithmetic and copies ran while one was open for 1% -> 1% of each run, Pallas kernels for 0% -> 3%
where the time goes in v2:
time: 71 us; the launch traced here: 70.7 us
  blocking collectives  23.2 us (33%)
  starting transfers between devices  20.9 us (29%)
  waiting for transfers between devices  13.8 us (19%)
  Pallas kernels  10.7 us (15%)
  local copies, waits for them, and re-layouts  1.77 us (2%)
    all_to_all x1, blocking collectives, local(): lax.all_to_all(mixed.reshape(S, F, rows, L), 'sub', split_axis=0, concat_...  23.2 us
    pallas_call x6, Pallas kernels, kernel(): pl.pallas_call(body, out_shape=out, in_specs=specs, out_specs=(out_specs,...  10.7 us
    all_to_all x1, starting transfers between devices, local(): lax.all_to_all(chunks, 'sub', split_axis=0, concat_axis=0, tiled=True)  6.22 us
    ppermute x1, starting transfers between devices, local(): above = lax.ppermute(down, 'tile', forth)  5.43 us
    ppermute x1, starting transfers between devices, local(): terrain_above = lax.ppermute(down, 'tile', forth)  5.43 us
    all_to_all x1, waiting for transfers between devices, local(): lax.all_to_all(chunks, 'sub', split_axis=0, concat_axis=0, tiled=True)  5.43 us
    ppermute x1, waiting for transfers between devices, local(): above = lax.ppermute(down, 'tile', forth)  5.18 us
    ppermute x1, waiting for transfers between devices, local(): below = lax.ppermute(up, 'tile', back)  3.21 us
  transfers between devices with their start and end apart: 5, of which 3 were waited for; matrix products, arithmetic and copies ran while one was open for 1% of the time, Pallas kernels for 3%

profile of v2, /device:TPU:249, one launch (start us, length us, event | category | flops | bytes accessed | tf_op | source)
XLA Modules:
  0.0 70.7 jit_solution(8124951403887590262)
XLA Ops:
  0.0 0.0 copy-start.1
  0.0 1.1 %copy-done.1 = f32[1,3,32,2048]{3,2,1,0:T(8,128)S(1)} copy-done((f32[1,3,32,2048]{3,2,1,0:T(8,128)S(1)}, f32[1,3,32,2048]{3,2,1,0:T(8,128)}, u32[]{:S(2)}) %copy-start.1) | copy-done | bytes 786456
  1.1 1.2 %shard_map.55 = f32[16,14,8,128]{3,2,1,0:T(8,128)} custom-call(f32[3,32,2048]{2,1,0:T(8,128)S(1)} %bitcast.12), custom_call_target="tpu_custom_call" | custom-call | tf_op jit(solution)/shard_map/pallas_call | solution.py:282
  2.3 0.0 copy-start
  2.3 6.2 %all-to-all-start = ((f32[16,14,8,128]{3,2,1,0:T(8,128)}), f32[16,14,8,128]{3,2,1,0:T(8,128)S(1)}, u32[]{:S(2)}, u32[]{:S(2)}) async-start(f32[16,14,8,128]{3,2,1,0:T(8,128)} %shard_map.55), calls=%async_computation | async-start | bytes 1835008 | tf_op jit(solution)/shard_map/all_to_all | solution.py:306
  8.6 0.1 pad_add_fusion.place_ref
  8.6 0.0 copy-done
  8.6 0.6 shard_map.57
  9.2 5.4 %collective-permute-start.2 = (s32[2,8,128]{2,1,0:T(8,128)S(1)}, s32[2,8,128]{2,1,0:T(8,128)S(1)}, u32[]{:S(2)}, u32[]{:S(2)}) collective-permute-start(s32[2,8,128]{2,1,0:T(8,128)S(1)} %get-tuple-element.11), channel_id=1, source_target_pairs={{0,1},{1,2},{2,3},{3,4},{4,5},{5,6},{6,7},{7,8},{8,9},{9,10},{10,1... | collective-permute-start | bytes 24584 | tf_op jit(solution)/shard_map/ppermute | solution.py:310
  14.6 0.0 copy-start.2
  14.6 1.9 %collective-permute-start.3 = (s32[2,8,128]{2,1,0:T(8,128)S(1)}, s32[2,8,128]{2,1,0:T(8,128)S(1)}, u32[]{:S(2)}, u32[]{:S(2)}) collective-permute-start(s32[2,8,128]{2,1,0:T(8,128)S(1)} %get-tuple-element.12), channel_id=1, source_target_pairs={{1,0},{2,1},{3,2},{4,3},{5,4},{6,5},{7,6},{8,7},{9,8},{10,9},{11,1... | collective-permute-start | bytes 24584 | tf_op jit(solution)/shard_map/ppermute | solution.py:311
  16.6 5.4 %all-to-all-done.x_ref = f32[16,14,8,128]{3,2,1,0:T(8,128)S(1)} async-done(((f32[16,14,8,128]{3,2,1,0:T(8,128)}), f32[16,14,8,128]{3,2,1,0:T(8,128)S(1)}, u32[]{:S(2)}, u32[]{:S(2)}) %all-to-all-start) | async-done | bytes 917536 | tf_op jit(solution)/shard_map/all_to_all | solution.py:306
  22.0 0.0 copy-done.2
  22.0 0.0 copy-start.4
  22.0 0.8 %shard_map.56 = (f32[56,8,128]{2,1,0:T(8,128)S(1)}, f32[56,8,128]{2,1,0:T(8,128)S(1)}) custom-call(s32[3]{0:T(128)S(1)} %pad_add_fusion.place_ref, f32[8]{0:T(128)S(1)} %copy-done.2, f32[16,14,8,128]{3,2,1,0:T(8,128)S(1)} %all-to-all-done.x_ref, s32[32,2048]{1,0:T(8,128)S(1)} %copy-done), custom_call_target="tpu_custom_call" | custom-call | tf_op jit(solution)/shard_map/pallas_call | solution.py:282
  22.8 5.4 %collective-permute-start = (f32[56,8,128]{2,1,0:T(8,128)S(1)}, f32[56,8,128]{2,1,0:T(8,128)S(1)}, u32[]{:S(2)}, u32[]{:S(2)}) collective-permute-start(f32[56,8,128]{2,1,0:T(8,128)S(1)} %get-tuple-element.9), channel_id=1, source_target_pairs={{0,1},{1,2},{2,3},{3,4},{4,5},{5,6},{6,7},{7,8},{8,9},{9,10},{10,1... | collective-permute-start | bytes 688136 | tf_op jit(solution)/shard_map/ppermute | solution.py:325
  28.2 1.9 %collective-permute-start.1 = (f32[56,8,128]{2,1,0:T(8,128)S(1)}, f32[56,8,128]{2,1,0:T(8,128)S(1)}, u32[]{:S(2)}, u32[]{:S(2)}) collective-permute-start(f32[56,8,128]{2,1,0:T(8,128)S(1)} %get-tuple-element.10), channel_id=1, source_target_pairs={{1,0},{2,1},{3,2},{4,3},{5,4},{6,5},{7,6},{8,7},{9,8},{10,9},{11,1... | collective-permute-start | bytes 688136 | tf_op jit(solution)/shard_map/ppermute | solution.py:326
  30.2 0.0 copy-done.4
  30.2 0.1 broadcast_multiply_fusion
  30.3 0.0 copy-start.3
  30.3 0.2 mul.31.weights_ref
  30.5 0.0 collective-permute-done.2.above_ref
  30.5 0.0 collective-permute-done.3.below_ref
  30.5 0.4 copy-done.3
  30.9 1.0 %shard_map.58.coef_ref = f32[2,6,160,128]{3,2,1,0:T(8,128)S(1)} custom-call(s32[3]{0:T(128)S(1)} %pad_add_fusion.place_ref, f32[8]{0:T(128)S(1)} %copy-done.2, f32[8]{0:T(128)S(1)} %copy-done.3, s32[32,2048]{1,0:T(8,128)S(1)} %copy-done, s32[2,8,128]{2,1,0:T(8,128)S(1)} %collective-permute-done.2.above_ref, s32[2,8,128]{2,1,0:T(8,128)S(1)} %collective-permute-done.3.below_ref), custom_call_target="tpu_custom_call" | custom-call | tf_op jit(solution)/shard_map/pallas_call | solution.py:282
  31.9 5.2 %collective-permute-done = f32[56,8,128]{2,1,0:T(8,128)S(1)} collective-permute-done((f32[56,8,128]{2,1,0:T(8,128)S(1)}, f32[56,8,128]{2,1,0:T(8,128)S(1)}, u32[]{:S(2)}, u32[]{:S(2)}) %collective-permute-start) | collective-permute-done | bytes 229408 | tf_op jit(solution)/shard_map/ppermute | solution.py:325
  37.1 3.2 %collective-permute-done.1 = f32[56,8,128]{2,1,0:T(8,128)S(1)} collective-permute-done((f32[56,8,128]{2,1,0:T(8,128)S(1)}, f32[56,8,128]{2,1,0:T(8,128)S(1)}, u32[]{:S(2)}, u32[]{:S(2)}) %collective-permute-start.1) | collective-permute-done | bytes 229408 | tf_op jit(solution)/shard_map/ppermute | solution.py:326
  40.3 6.2 %shard_map.59 = f32[1536,128]{1,0:T(8,128)S(1)} custom-call(s32[3]{0:T(128)S(1)} %pad_add_fusion.place_ref, f32[1792,128]{1,0:T(8,128)S(1)} %bitcast.10, f32[448,128]{1,0:T(8,128)S(1)} %bitcast.13, f32[448,128]{1,0:T(8,128)S(1)} %bitcast.14, f32[2,6,160,128]{3,2,1,0:T(8,128)S(1)} %shard_map.58.coef_ref, f32[128,128]{1,0:T(8,128)S(1)} %mul.31.weights_ref), custom_call_target="tpu_custom_call" | custom-call | tf_op jit(solution)/shard_map/pallas_call | solution.py:282
  46.5 23.2 %all_to_all.10.x_ref = f32[16,3,32,128]{3,2,1,0:T(8,128)S(1)} all-to-all(f32[16,3,32,128]{3,2,1,0:T(8,128)S(1)} %bitcast.11), channel_id=1, replica_groups=mesh['sub'=16,'tile'=32] {'sub'}, dimensions={0} | all-to-all | bytes 1572864 | tf_op jit(solution)/shard_map/all_to_all | solution.py:348
  69.7 1.0 %shard_map.60 = f32[3,32,2048]{2,1,0:T(8,128)} custom-call(f32[16,3,32,128]{3,2,1,0:T(8,128)S(1)} %all_to_all.10.x_ref), custom_call_target="tpu_custom_call" | custom-call | tf_op jit(solution)/shard_map/pallas_call | solution.py:282
  (1 shorter events, 0.0 us)
Async XLA Ops:
  0.0 1.1 %copy-start.1 = (f32[1,3,32,2048]{3,2,1,0:T(8,128)S(1)}, f32[1,3,32,2048]{3,2,1,0:T(8,128)}, u32[]{:S(2)}) copy-start(f32[1,3,32,2048]{3,2,1,0:T(8,128)} %param.5) | copy-start | bytes 2359300
  2.3 6.3 %copy-start = (s32[32,2048]{1,0:T(8,128)S(1)}, s32[32,2048]{1,0:T(8,128)}, u32[]{:S(2)}) copy-start(s32[32,2048]{1,0:T(8,128)} %ter_ref.5) | copy-start | bytes 786436
  2.3 19.7 %all-to-all-start = ((f32[16,14,8,128]{3,2,1,0:T(8,128)}), f32[16,14,8,128]{3,2,1,0:T(8,128)S(1)}, u32[]{:S(2)}, u32[]{:S(2)}) async-start(f32[16,14,8,128]{3,2,1,0:T(8,128)} %shard_map.55), calls=%async_computation | async-start | bytes 1835008 | tf_op jit(solution)/shard_map/all_to_all | solution.py:306
  9.2 21.3 %collective-permute-start.2 = (s32[2,8,128]{2,1,0:T(8,128)S(1)}, s32[2,8,128]{2,1,0:T(8,128)S(1)}, u32[]{:S(2)}, u32[]{:S(2)}) collective-permute-start(s32[2,8,128]{2,1,0:T(8,128)S(1)} %get-tuple-element.11), channel_id=1, source_target_pairs={{0,1},{1,2},{2,3},{3,4},{4,5},{5,6},{6,7},{7,8},{8,9},{9,10},{10,1... | collective-permute-start | bytes 24584 | tf_op jit(solution)/shard_map/ppermute | solution.py:310
  14.6 7.4 %copy-start.2 = (f32[8]{0:T(128)S(1)}, f32[8]{0:T(128)}, u32[]{:S(2)}) copy-start(f32[8]{0:T(128)} %depth_ref.3) | copy-start | bytes 100
  14.6 15.9 %collective-permute-start.3 = (s32[2,8,128]{2,1,0:T(8,128)S(1)}, s32[2,8,128]{2,1,0:T(8,128)S(1)}, u32[]{:S(2)}, u32[]{:S(2)}) collective-permute-start(s32[2,8,128]{2,1,0:T(8,128)S(1)} %get-tuple-element.12), channel_id=1, source_target_pairs={{1,0},{2,1},{3,2},{4,3},{5,4},{6,5},{7,6},{8,7},{9,8},{10,9},{11,1... | collective-permute-start | bytes 24584 | tf_op jit(solution)/shard_map/ppermute | solution.py:311
  22.0 8.2 %copy-start.4 = (f32[16,16]{1,0:T(8,128)S(1)}, f32[16,16]{1,0:T(8,128)}, u32[]{:S(2)}) copy-start(f32[16,16]{1,0:T(8,128)} %param.9) | copy-start | bytes 3076
  22.8 14.3 %collective-permute-start = (f32[56,8,128]{2,1,0:T(8,128)S(1)}, f32[56,8,128]{2,1,0:T(8,128)S(1)}, u32[]{:S(2)}, u32[]{:S(2)}) collective-permute-start(f32[56,8,128]{2,1,0:T(8,128)S(1)} %get-tuple-element.9), channel_id=1, source_target_pairs={{0,1},{1,2},{2,3},{3,4},{4,5},{5,6},{6,7},{7,8},{8,9},{9,10},{10,1... | collective-permute-start | bytes 688136 | tf_op jit(solution)/shard_map/ppermute | solution.py:325
  28.2 12.1 %collective-permute-start.1 = (f32[56,8,128]{2,1,0:T(8,128)S(1)}, f32[56,8,128]{2,1,0:T(8,128)S(1)}, u32[]{:S(2)}, u32[]{:S(2)}) collective-permute-start(f32[56,8,128]{2,1,0:T(8,128)S(1)} %get-tuple-element.10), channel_id=1, source_target_pairs={{1,0},{2,1},{3,2},{4,3},{5,4},{6,5},{7,6},{8,7},{9,8},{10,9},{11,1... | collective-permute-start | bytes 688136 | tf_op jit(solution)/shard_map/ppermute | solution.py:326
  30.3 0.7 copy-start.3

commit v3 on v2

--- a/solution.py
+++ b/solution.py
@@ -39,23 +39,34 @@
     return value
 
 
-def pack_kernel(x_ref, o_ref):
+def pack_kernel(x_hbm, o_ref, x_s, sems):
     lane = iota(1)
+    copies = [
+        [
+            pltpu.make_async_copy(
+                x_hbm.at[f, pl.ds(8 * g, 8)], x_s.at[f, pl.ds(8 * g, 8)], sems.at[f, g]
+            )
+            for f in range(F)
+        ]
+        for g in range(G)
+    ]
+    for copy in sum(copies, []):
+        copy.start()
 
     def tile(f, g, c):
-        return x_ref[f, 8 * g : 8 * g + 8, L * (c % S) : L * (c % S) + L]
-
-    for c in range(S):
-        for f in range(F):
-            for g in range(G):
+        return x_s[f, 8 * g : 8 * g + 8, L * (c % S) : L * (c % S) + L]
+
+    for j in range(2):
+        for copy in copies[2 * j] + copies[2 * j + 1]:
+            copy.wait()
+        for c in range(S):
+            packed = jnp.zeros((8, L), F32)
+            for q in reversed(range(6)):
+                f, g = q % 3, 2 * j + q // 3
                 o_ref[c, f * G + g] = tile(f, g, c)
-        for j in range(2):
-            packed = jnp.zeros((8, L), F32)
-            for q in range(6):
-                f, g = q % 3, 2 * j + q // 3
                 sides = jnp.where(lane < 64, tile(f, g, c + 1), tile(f, g, c - 1))
                 sides = pltpu.roll(sides, W * q + C, 1)
-                packed = jnp.where((lane >= W * q) & (lane < W * q + W), sides, packed)
+                packed = jnp.where(lane < W * q + W, sides, packed)
             o_ref[c, NMAIN + j] = packed
 
 
@@ -250,16 +261,21 @@
         spread(buffers[step % 2], buffers[(step + 1) % 2])
     smooth = buffers[DSTEPS % 2]
 
-    weights = weights_ref[...]
+    def halves(value):
+        high = value.astype(jnp.bfloat16)
+        return high, (value - high.astype(F32)).astype(jnp.bfloat16)
+
+    def product(left, right):
+        return lax.dot_general(
+            left, right, (((1,), (1,)), ((), ())), preferred_element_type=F32
+        )
+
+    high, low = halves(weights_ref[...])
+    twice = jnp.concatenate([high, high], axis=1)
     for f in range(F):
         for r in range(DEPTH):
-            mixed = lax.dot_general(
-                weights,
-                smooth[f, r, EDGE : EDGE + L, :],
-                (((1,), (1,)), ((), ())),
-                precision=lax.Precision.HIGHEST,
-                preferred_element_type=F32,
-            )
+            parts = halves(smooth[f, r, EDGE : EDGE + L, :])
+            mixed = product(twice, jnp.concatenate(parts, axis=1)) + product(low, parts[0])
             for b in range(BLOCKS):
                 row = row_of(b, r)
                 if 0 <= row < 8 * G:
@@ -302,7 +318,17 @@
     forth = [(i, i + 1) for i in range(strips - 1)]
     back = [(j, i) for i, j in forth]
 
-    chunks = kernel(pack_kernel, pltpu.VMEM((S, NALL, 8, L), F32), (states[0],))
+    chunks = pl.pallas_call(
+        pack_kernel,
+        out_shape=pltpu.VMEM((S, NALL, 8, L), F32),
+        in_specs=[pl.BlockSpec(memory_space=pltpu.HBM)],
+        out_specs=VMEM,
+        scratch_shapes=[
+            pltpu.VMEM((F, rows, S * L), F32),
+            pltpu.SemaphoreType.DMA((F, G)),
+        ],
+        compiler_params=pltpu.CompilerParams(vmem_limit_bytes=12 * 2**20),
+    )(pltpu.with_memory_space_constraint(states[0], pltpu.HBM))
     held = lax.all_to_all(chunks, "sub", split_axis=0, concat_axis=0, tiled=True)
 
     edge = pltpu.VMEM((2, 8, L), jnp.int32)

time: 71 us -> 70 us (0.986)
  local copies, waits for them, and re-layouts: 1.77 us -> 0.64 us
    pallas_call x0 -> x1, Pallas kernels: none -> 2.4 us  [local(): pl.pallas_call(pack_kernel, out_shape=pltpu.VMEM((S, NALL, 8, L), F32), i...]
    pallas_call x6 -> x5, Pallas kernels: 10.7 us -> 8.35 us  [kernel(): pl.pallas_call(body, out_shape=out, in_specs=specs, out_specs=(out_specs,...]
    unnamed x10 -> x8, local copies, waits for them, and re-layouts: 1.58 us -> 0.45 us
where the time goes in v3:
time: 70 us; the launch traced here: 69.6 us
  blocking collectives  23.2 us (33%)
  starting transfers between devices  20.9 us (30%)
  waiting for transfers between devices  13.8 us (20%)
  Pallas kernels  10.8 us (15%)
    all_to_all x1, blocking collectives, local(): lax.all_to_all(mixed.reshape(S, F, rows, L), 'sub', split_axis=0, concat_...  23.2 us
    pallas_call x5, Pallas kernels, kernel(): pl.pallas_call(body, out_shape=out, in_specs=specs, out_specs=(out_specs,...  8.35 us
    all_to_all x1, starting transfers between devices, local(): lax.all_to_all(chunks, 'sub', split_axis=0, concat_axis=0, tiled=True)  6.24 us
    ppermute x1, starting transfers between devices, local(): terrain_above = lax.ppermute(down, 'tile', forth)  5.43 us
    ppermute x1, starting transfers between devices, local(): above = lax.ppermute(down, 'tile', forth)  5.43 us
    all_to_all x1, waiting for transfers between devices, local(): lax.all_to_all(chunks, 'sub', split_axis=0, concat_axis=0, tiled=True)  5.43 us
    ppermute x1, waiting for transfers between devices, local(): above = lax.ppermute(down, 'tile', forth)  5.18 us
    ppermute x1, waiting for transfers between devices, local(): below = lax.ppermute(up, 'tile', back)  3.21 us
  transfers between devices with their start and end apart: 5, of which 3 were waited for; matrix products, arithmetic and copies ran while one was open for 1% of the time, Pallas kernels for 3%

profile of v3, /device:TPU:249, one launch (start us, length us, event | category | flops | bytes accessed | tf_op | source)
XLA Modules:
  0.0 69.6 jit_solution(3294002717038988624)
XLA Ops:
  0.0 2.4 %shard_map.55 = f32[16,14,8,128]{3,2,1,0:T(8,128)} custom-call(f32[3,32,2048]{2,1,0:T(8,128)} %bitcast.14), custom_call_target="tpu_custom_call" | custom-call | tf_op jit(solution)/shard_map/pallas_call | solution.py:321
  2.4 0.0 copy-start
  2.4 6.2 %all-to-all-start = ((f32[16,14,8,128]{3,2,1,0:T(8,128)}), f32[16,14,8,128]{3,2,1,0:T(8,128)S(1)}, u32[]{:S(2)}, u32[]{:S(2)}) async-start(f32[16,14,8,128]{3,2,1,0:T(8,128)} %shard_map.55), calls=%async_computation | async-start | bytes 1835008 | tf_op jit(solution)/shard_map/all_to_all | solution.py:332
  8.7 0.1 pad_add_fusion.place_ref
  8.7 0.0 copy-done
  8.7 0.6 shard_map.57
  9.3 5.4 %collective-permute-start.2 = (s32[2,8,128]{2,1,0:T(8,128)S(1)}, s32[2,8,128]{2,1,0:T(8,128)S(1)}, u32[]{:S(2)}, u32[]{:S(2)}) collective-permute-start(s32[2,8,128]{2,1,0:T(8,128)S(1)} %get-tuple-element.11), channel_id=1, source_target_pairs={{0,1},{1,2},{2,3},{3,4},{4,5},{5,6},{6,7},{7,8},{8,9},{9,10},{10,1... | collective-permute-start | bytes 24584 | tf_op jit(solution)/shard_map/ppermute | solution.py:336
  14.7 0.0 copy-start.1
  14.7 1.9 %collective-permute-start.3 = (s32[2,8,128]{2,1,0:T(8,128)S(1)}, s32[2,8,128]{2,1,0:T(8,128)S(1)}, u32[]{:S(2)}, u32[]{:S(2)}) collective-permute-start(s32[2,8,128]{2,1,0:T(8,128)S(1)} %get-tuple-element.12), channel_id=1, source_target_pairs={{1,0},{2,1},{3,2},{4,3},{5,4},{6,5},{7,6},{8,7},{9,8},{10,9},{11,1... | collective-permute-start | bytes 24584 | tf_op jit(solution)/shard_map/ppermute | solution.py:337
  16.7 5.4 %all-to-all-done.x_ref = f32[16,14,8,128]{3,2,1,0:T(8,128)S(1)} async-done(((f32[16,14,8,128]{3,2,1,0:T(8,128)}), f32[16,14,8,128]{3,2,1,0:T(8,128)S(1)}, u32[]{:S(2)}, u32[]{:S(2)}) %all-to-all-start) | async-done | bytes 917536 | tf_op jit(solution)/shard_map/all_to_all | solution.py:332
  22.1 0.0 copy-done.1
  22.1 0.0 copy-start.3
  22.1 0.8 %shard_map.56 = (f32[56,8,128]{2,1,0:T(8,128)S(1)}, f32[56,8,128]{2,1,0:T(8,128)S(1)}) custom-call(s32[3]{0:T(128)S(1)} %pad_add_fusion.place_ref, f32[8]{0:T(128)S(1)} %copy-done.1, f32[16,14,8,128]{3,2,1,0:T(8,128)S(1)} %all-to-all-done.x_ref, s32[32,2048]{1,0:T(8,128)S(1)} %copy-done), custom_call_target="tpu_custom_call" | custom-call | tf_op jit(solution)/shard_map/pallas_call | solution.py:298
  22.9 5.4 %collective-permute-start = (f32[56,8,128]{2,1,0:T(8,128)S(1)}, f32[56,8,128]{2,1,0:T(8,128)S(1)}, u32[]{:S(2)}, u32[]{:S(2)}) collective-permute-start(f32[56,8,128]{2,1,0:T(8,128)S(1)} %get-tuple-element.9), channel_id=1, source_target_pairs={{0,1},{1,2},{2,3},{3,4},{4,5},{5,6},{6,7},{7,8},{8,9},{9,10},{10,1... | collective-permute-start | bytes 688136 | tf_op jit(solution)/shard_map/ppermute | solution.py:351
  28.3 1.9 %collective-permute-start.1 = (f32[56,8,128]{2,1,0:T(8,128)S(1)}, f32[56,8,128]{2,1,0:T(8,128)S(1)}, u32[]{:S(2)}, u32[]{:S(2)}) collective-permute-start(f32[56,8,128]{2,1,0:T(8,128)S(1)} %get-tuple-element.10), channel_id=1, source_target_pairs={{1,0},{2,1},{3,2},{4,3},{5,4},{6,5},{7,6},{8,7},{9,8},{10,9},{11,1... | collective-permute-start | bytes 688136 | tf_op jit(solution)/shard_map/ppermute | solution.py:352
  30.3 0.0 copy-done.3
  30.3 0.1 broadcast_multiply_fusion
  30.4 0.0 copy-start.2
  30.4 0.2 mul.31.weights_ref
  30.6 0.0 collective-permute-done.2.above_ref
  30.6 0.0 collective-permute-done.3.below_ref
  30.6 0.4 copy-done.2
  31.0 1.0 %shard_map.58.coef_ref = f32[2,6,160,128]{3,2,1,0:T(8,128)S(1)} custom-call(s32[3]{0:T(128)S(1)} %pad_add_fusion.place_ref, f32[8]{0:T(128)S(1)} %copy-done.1, f32[8]{0:T(128)S(1)} %copy-done.2, s32[32,2048]{1,0:T(8,128)S(1)} %copy-done, s32[2,8,128]{2,1,0:T(8,128)S(1)} %collective-permute-done.2.above_ref, s32[2,8,128]{2,1,0:T(8,128)S(1)} %collective-permute-done.3.below_ref), custom_call_target="tpu_custom_call" | custom-call | tf_op jit(solution)/shard_map/pallas_call | solution.py:298
  32.0 5.2 %collective-permute-done = f32[56,8,128]{2,1,0:T(8,128)S(1)} collective-permute-done((f32[56,8,128]{2,1,0:T(8,128)S(1)}, f32[56,8,128]{2,1,0:T(8,128)S(1)}, u32[]{:S(2)}, u32[]{:S(2)}) %collective-permute-start) | collective-permute-done | bytes 229408 | tf_op jit(solution)/shard_map/ppermute | solution.py:351
  37.2 3.2 %collective-permute-done.1 = f32[56,8,128]{2,1,0:T(8,128)S(1)} collective-permute-done((f32[56,8,128]{2,1,0:T(8,128)S(1)}, f32[56,8,128]{2,1,0:T(8,128)S(1)}, u32[]{:S(2)}, u32[]{:S(2)}) %collective-permute-start.1) | collective-permute-done | bytes 229408 | tf_op jit(solution)/shard_map/ppermute | solution.py:352
  40.4 5.0 %shard_map.59 = f32[1536,128]{1,0:T(8,128)S(1)} custom-call(s32[3]{0:T(128)S(1)} %pad_add_fusion.place_ref, f32[1792,128]{1,0:T(8,128)S(1)} %bitcast.10, f32[448,128]{1,0:T(8,128)S(1)} %bitcast.12, f32[448,128]{1,0:T(8,128)S(1)} %bitcast.13, f32[2,6,160,128]{3,2,1,0:T(8,128)S(1)} %shard_map.58.coef_ref, f32[128,128]{1,0:T(8,128)S(1)} %mul.31.weights_ref), custom_call_target="tpu_custom_call" | custom-call | tf_op jit(solution)/shard_map/pallas_call | solution.py:298
  45.5 23.2 %all_to_all.10.x_ref = f32[16,3,32,128]{3,2,1,0:T(8,128)S(1)} all-to-all(f32[16,3,32,128]{3,2,1,0:T(8,128)S(1)} %bitcast.11), channel_id=1, replica_groups=mesh['sub'=16,'tile'=32] {'sub'}, dimensions={0} | all-to-all | bytes 1572864 | tf_op jit(solution)/shard_map/all_to_all | solution.py:374
  68.6 1.0 %shard_map.60 = f32[3,32,2048]{2,1,0:T(8,128)} custom-call(f32[16,3,32,128]{3,2,1,0:T(8,128)S(1)} %all_to_all.10.x_ref), custom_call_target="tpu_custom_call" | custom-call | tf_op jit(solution)/shard_map/pallas_call | solution.py:298
  (1 shorter events, 0.0 us)
Async XLA Ops:
  2.4 6.3 %copy-start = (s32[32,2048]{1,0:T(8,128)S(1)}, s32[32,2048]{1,0:T(8,128)}, u32[]{:S(2)}) copy-start(s32[32,2048]{1,0:T(8,128)} %ter_ref.5) | copy-start | bytes 786436
  2.4 19.7 %all-to-all-start = ((f32[16,14,8,128]{3,2,1,0:T(8,128)}), f32[16,14,8,128]{3,2,1,0:T(8,128)S(1)}, u32[]{:S(2)}, u32[]{:S(2)}) async-start(f32[16,14,8,128]{3,2,1,0:T(8,128)} %shard_map.55), calls=%async_computation | async-start | bytes 1835008 | tf_op jit(solution)/shard_map/all_to_all | solution.py:332
  9.3 21.3 %collective-permute-start.2 = (s32[2,8,128]{2,1,0:T(8,128)S(1)}, s32[2,8,128]{2,1,0:T(8,128)S(1)}, u32[]{:S(2)}, u32[]{:S(2)}) collective-permute-start(s32[2,8,128]{2,1,0:T(8,128)S(1)} %get-tuple-element.11), channel_id=1, source_target_pairs={{0,1},{1,2},{2,3},{3,4},{4,5},{5,6},{6,7},{7,8},{8,9},{9,10},{10,1... | collective-permute-start | bytes 24584 | tf_op jit(solution)/shard_map/ppermute | solution.py:336
  14.7 7.4 %copy-start.1 = (f32[8]{0:T(128)S(1)}, f32[8]{0:T(128)}, u32[]{:S(2)}) copy-start(f32[8]{0:T(128)} %depth_ref.3) | copy-start | bytes 100
  14.7 15.9 %collective-permute-start.3 = (s32[2,8,128]{2,1,0:T(8,128)S(1)}, s32[2,8,128]{2,1,0:T(8,128)S(1)}, u32[]{:S(2)}, u32[]{:S(2)}) collective-permute-start(s32[2,8,128]{2,1,0:T(8,128)S(1)} %get-tuple-element.12), channel_id=1, source_target_pairs={{1,0},{2,1},{3,2},{4,3},{5,4},{6,5},{7,6},{8,7},{9,8},{10,9},{11,1... | collective-permute-start | bytes 24584 | tf_op jit(solution)/shard_map/ppermute | solution.py:337
  22.1 8.2 %copy-start.3 = (f32[16,16]{1,0:T(8,128)S(1)}, f32[16,16]{1,0:T(8,128)}, u32[]{:S(2)}) copy-start(f32[16,16]{1,0:T(8,128)} %param.9) | copy-start | bytes 3076
  22.9 14.3 %collective-permute-start = (f32[56,8,128]{2,1,0:T(8,128)S(1)}, f32[56,8,128]{2,1,0:T(8,128)S(1)}, u32[]{:S(2)}, u32[]{:S(2)}) collective-permute-start(f32[56,8,128]{2,1,0:T(8,128)S(1)} %get-tuple-element.9), channel_id=1, source_target_pairs={{0,1},{1,2},{2,3},{3,4},{4,5},{5,6},{6,7},{7,8},{8,9},{9,10},{10,1... | collective-permute-start | bytes 688136 | tf_op jit(solution)/shard_map/ppermute | solution.py:351
  28.3 12.1 %collective-permute-start.1 = (f32[56,8,128]{2,1,0:T(8,128)S(1)}, f32[56,8,128]{2,1,0:T(8,128)S(1)}, u32[]{:S(2)}, u32[]{:S(2)}) collective-permute-start(f32[56,8,128]{2,1,0:T(8,128)S(1)} %get-tuple-element.10), channel_id=1, source_target_pairs={{1,0},{2,1},{3,2},{4,3},{5,4},{6,5},{7,6},{8,7},{9,8},{10,9},{11,1... | collective-permute-start | bytes 688136 | tf_op jit(solution)/shard_map/ppermute | solution.py:352
  30.4 0.7 copy-start.2

commit v4 on v3

--- a/solution.py
+++ b/solution.py
@@ -14,9 +14,10 @@
 R = 8
 C = 9
 W = 2 * C
-NMAIN = F * G
-NALL = NMAIN + 2
-NHALO = S * F + S // 2
+NOUTER = 2 * F + 1
+NINNER = 2 * F + 2
+NHALO = S * F + S // 2 + 1
+SPARE = 2 * F * W
 BLOCKS = 8
 DEPTH = 6
 EDGE = 16
@@ -39,35 +40,74 @@
     return value
 
 
-def pack_kernel(x_hbm, o_ref, x_s, sems):
+def fetch(pairs, sems):
+    copies = [pltpu.make_async_copy(src, dst, sems.at[i]) for i, (src, dst) in enumerate(pairs)]
+    for copy in copies:
+        copy.start()
+    for copy in copies:
+        copy.wait()
+
+
+def pack(o_ref, tile, packed_of):
     lane = iota(1)
-    copies = [
-        [
-            pltpu.make_async_copy(
-                x_hbm.at[f, pl.ds(8 * g, 8)], x_s.at[f, pl.ds(8 * g, 8)], sems.at[f, g]
-            )
-            for f in range(F)
-        ]
-        for g in range(G)
-    ]
-    for copy in sum(copies, []):
-        copy.start()
-
-    def tile(f, g, c):
-        return x_s[f, 8 * g : 8 * g + 8, L * (c % S) : L * (c % S) + L]
-
-    for j in range(2):
-        for copy in copies[2 * j] + copies[2 * j + 1]:
-            copy.wait()
-        for c in range(S):
-            packed = jnp.zeros((8, L), F32)
-            for q in reversed(range(6)):
-                f, g = q % 3, 2 * j + q // 3
-                o_ref[c, f * G + g] = tile(f, g, c)
-                sides = jnp.where(lane < 64, tile(f, g, c + 1), tile(f, g, c - 1))
-                sides = pltpu.roll(sides, W * q + C, 1)
-                packed = jnp.where(lane < W * q + W, sides, packed)
-            o_ref[c, NMAIN + j] = packed
+
+    def sides(q, c, at):
+        value = jnp.where(lane < 64, tile(q, (c + 1) % S), tile(q, (c - 1) % S))
+        return pltpu.roll(value, at + C, 1)
+
+    for c in range(S):
+        packed = packed_of(c, sides)
+        for q in reversed(range(2 * F)):
+            o_ref[c, q] = tile(q, c)
+            packed = jnp.where(lane < W * q + W, sides(q, c, W * q), packed)
+        o_ref[c, 2 * F] = packed
+
+
+def outer_kernel(depth_ref, x_hbm, ter_hbm, o_ref, x_s, ter_s, rows_s, sems):
+    row = iota(0, (8, S * L))
+    groups = [(1, 1), (1, 2), (0, 0), (0, 3), (1, 0), (1, 3), (2, 0), (2, 3)]
+    fetch(
+        [(ter_hbm.at[pl.ds(8, 16)], ter_s)]
+        + [(x_hbm.at[f, pl.ds(8 * g, 8)], x_s.at[f, g]) for f, g in groups],
+        sems,
+    )
+
+    def flux(g):
+        return lookup(ter_s[8 * g - 8 : 8 * g, :], depth_ref) * x_s[1, g]
+
+    rows_s[0] = x_s[0, 0] - jnp.where(row == 7, 0.25 * pltpu.roll(flux(1), 7, 0), 0.0)
+    rows_s[1] = x_s[0, 3] + jnp.where(row == 0, 0.25 * pltpu.roll(flux(2), 1, 0), 0.0)
+
+    def tile(q, c):
+        cols = slice(L * c, L * c + L)
+        if q % F == 0:
+            return rows_s[q // F, :, cols]
+        return x_s[q % F, q // F * (G - 1), :, cols]
+
+    pack(o_ref, tile, lambda c, sides: jnp.zeros((8, L), F32))
+
+
+def inner_kernel(x_hbm, o_ref, x_s, rows_s, sems):
+    row = iota(0, (8, S * L))
+    groups = [(0, 0), (0, 3)] + [(f, g) for f in range(F) for g in (1, 2)]
+    fetch([(x_hbm.at[f, pl.ds(8 * g, 8)], x_s.at[f, g]) for f, g in groups], sems)
+    rows_s[...] = jnp.where(row == 0, pltpu.roll(x_s[0, 0], 1, 0), pltpu.roll(x_s[0, 3], 1, 0))
+
+    def tile(q, c):
+        cols = slice(L * c, L * c + L)
+        if q == 2 * F:
+            return rows_s[:, cols]
+        return x_s[q % F, 1 + q // F, :, cols]
+
+    def packed_of(c, sides):
+        o_ref[c, 2 * F + 1] = tile(2 * F, c)
+        return sides(2 * F, c, SPARE)
+
+    pack(o_ref, tile, packed_of)
+
+
+def follow_kernel(x_ref, after_ref, o_ref):
+    pass
 
 
 def terrain_tiles(ter_ref, chunk, g):
@@ -78,38 +118,29 @@
     return tile(chunk), jnp.where(iota(1) < 64, tile(chunk + 1), tile(chunk - 1))
 
 
-def edge_kernel(place_ref, depth_ref, x_ref, ter_ref, up_ref, down_ref):
-    lane, row = iota(1), iota(0)
-    chunk = place_ref[0]
-
-    def send(o_ref, g, inner, edge, turn, sign, halo, flux_at, height_at, low_by, high_by):
-        own, sides = terrain_tiles(ter_ref, chunk, inner)
-        depth_own = sign * lookup(own, depth_ref)
-        depth_sides = pltpu.roll(sign * lookup(sides, depth_ref), W * flux_at + C, 1)
-        at_edge = row == edge
-        at_height = at_edge & (lane >= W * height_at) & (lane < W * height_at + W)
-        by = (W * (height_at - flux_at)) % L
-        packed = []
+def edge_kernel(place_ref, outer_ref, ter_ref, up_ref, down_ref):
+    lane = iota(1)
+
+    def send(o_ref, base, g, low_by, high_by):
+        own, sides = terrain_tiles(ter_ref, place_ref[0], g)
+        o_ref[NHALO - 1] = own.astype(F32)
+        sides = pltpu.roll(sides.astype(F32), SPARE + C, 1)
         for t in range(S):
-            flux = pltpu.roll(depth_own * x_ref[t, G + inner], turn, 0)
-            o_ref[t * F] = x_ref[t, g] + jnp.where(at_edge, flux, 0.0)
-            o_ref[t * F + 1] = x_ref[t, G + g]
-            o_ref[t * F + 2] = x_ref[t, 2 * G + g]
-            columns = x_ref[t, NMAIN + halo]
-            flux = pltpu.roll(pltpu.roll(depth_sides * columns, by, 1), turn, 0)
-            columns = columns + jnp.where(at_height, flux, 0.0)
-            shift = low_by if t < S // 2 else high_by
-            packed.append(pltpu.roll(columns, shift, 1) if shift else columns)
+            for f in range(F):
+                o_ref[t * F + f] = outer_ref[t, base + f]
+
+        def turned(t, by):
+            value = outer_ref[t, 2 * F]
+            return pltpu.roll(value, by, 1) if by else value
+
         for j in range(S // 2):
-            o_ref[S * F + j] = jnp.where(lane < 3 * W, packed[j], packed[j + S // 2])
-
-    send(up_ref, 0, 1, 7, 7, -0.25, 0, 4, 0, 0, 3 * W)
-    send(down_ref, 3, 2, 0, 1, 0.25, 1, 1, 3, L - 3 * W, 0)
-
-
-def terrain_kernel(place_ref, ter_ref, up_ref, down_ref):
-    up_ref[0], up_ref[1] = terrain_tiles(ter_ref, place_ref[0], 0)
-    down_ref[0], down_ref[1] = terrain_tiles(ter_ref, place_ref[0], G - 1)
+            columns = jnp.where(
+                lane < 3 * W, turned(j, low_by), turned(j + S // 2, high_by)
+            )
+            o_ref[S * F + j] = jnp.where(lane < SPARE, columns, sides)
+
+    send(up_ref, 0, 0, 0, 3 * W)
+    send(down_ref, F, G - 1, L - 3 * W, 0)
 
 
 def row_of(block, r):
@@ -124,9 +155,13 @@
 def coef_kernel(place_ref, depth_ref, spread_ref, ter_ref, above_ref, below_ref, o_ref, table_s):
     chunk, first, total = place_ref[0], place_ref[1], place_ref[2]
     lane = iota(1)
-    tiles = [(above_ref[0], above_ref[1])]
+
+    def beside(ref):
+        return ref[NHALO - 1], pltpu.roll(ref[S * F], L - SPARE - C, 1)
+
+    tiles = [beside(above_ref)]
     tiles += [terrain_tiles(ter_ref, chunk, g) for g in range(G)]
-    tiles += [(below_ref[0], below_ref[1])]
+    tiles += [beside(below_ref)]
     for i, (own, sides) in enumerate(tiles):
         rows = slice(8 * i, 8 * i + 8)
         table_s[0, rows] = lookup(own, depth_ref)
@@ -155,7 +190,7 @@
 
 
 def main_kernel(
-    place_ref, x_ref, above_ref, below_ref, coef_ref, weights_ref, o_ref,
+    place_ref, outer_ref, inner_ref, above_ref, below_ref, coef_ref, weights_ref, o_ref,
     a_s, b_s, flux_s, slope_s,
 ):
     first, total = place_ref[1], place_ref[2]
@@ -169,21 +204,41 @@
     for r in range(DEPTH):
         slope_s[r] = -0.25 * inside_of(first, total, r, (PART, L))
 
+    def outer_rows(at):
+        return outer_ref[pl.ds(at, S, 8 * NOUTER), :]
+
+    def inner_rows(at):
+        return inner_ref[pl.ds(at, S, 8 * NINNER), :]
+
     def main_rows(f, row):
         if row < 0:
             return above_ref[pl.ds(8 * f + row + R, S, 8 * F), :]
-        if row < 8 * G:
-            return x_ref[pl.ds(8 * G * f + row, S, 8 * NALL), :]
-        return below_ref[pl.ds(8 * f + row - 8 * G, S, 8 * F), :]
+        if row >= 8 * G:
+            return below_ref[pl.ds(8 * f + row - 8 * G, S, 8 * F), :]
+        if f == 0 and row in (7, 24):
+            return inner_rows(8 * 7 + row // 8 // 3)
+        if 8 <= row < 24:
+            return inner_rows(8 * ((row // 8 - 1) * F + f) + row % 8)
+        return outer_rows(8 * (row // 24 * F + f) + row % 8)
 
     def side_rows(row):
-        if 0 <= row < 8 * G:
-            g = row // 8
-            value = x_ref[pl.ds(8 * (NMAIN + g // 2) + row % 8, S, 8 * NALL), :]
-            return pltpu.roll(value, L - 3 * W, 1) if g % 2 else value
-        ref, at = (above_ref, row + R) if row < 0 else (below_ref, row - 8 * G)
-        value = ref[pl.ds(8 * S * F + at, S // 2, 8), :]
-        return jnp.concatenate([value, pltpu.roll(value, L - 3 * W, 1)], axis=0)
+        def turned(value, by):
+            return pltpu.roll(value, L - by, 1)
+
+        if not 0 <= row < 8 * G:
+            ref, at = (above_ref, row + R) if row < 0 else (below_ref, row - 8 * G)
+            value = ref[pl.ds(8 * S * F + at, S // 2, 8), :]
+            return jnp.concatenate([value, turned(value, 3 * W)], axis=0)
+        if 8 <= row < 24:
+            value = inner_rows(8 * 6 + row % 8)
+            return turned(value, 3 * W) if row >= 16 else value
+        value = outer_rows(8 * 6 + row % 8)
+        if row >= 24:
+            value = turned(value, 3 * W)
+        if row in (7, 24):
+            height = turned(inner_rows(8 * 6 + row // 8 // 3), SPARE)
+            value = jnp.where(lane < W, height, value)
+        return value
 
     for r in range(DEPTH):
         for f in range(F):
@@ -279,7 +334,7 @@
             for b in range(BLOCKS):
                 row = row_of(b, r)
                 if 0 <= row < 8 * G:
-                    o_ref[pl.ds(8 * G * f + row, S, 8 * NMAIN), :] = mixed[S * b : S * b + S]
+                    o_ref[pl.ds(8 * G * f + row, S, 8 * G * F), :] = mixed[S * b : S * b + S]
 
 
 def unpack_kernel(x_ref, o_ref, sems):
@@ -293,7 +348,7 @@
         copy.wait()
 
 
-def kernel(body, out, operands, scalars=0, scratch=(), out_specs=VMEM):
+def kernel(body, out, operands, scalars=0, scratch=(), out_specs=VMEM, cost=None):
     specs = [SMEM] * scalars + [VMEM] * (len(operands) - scalars)
     return pl.pallas_call(
         body,
@@ -301,12 +356,17 @@
         in_specs=specs,
         out_specs=(out_specs,) * len(out) if isinstance(out, tuple) else out_specs,
         scratch_shapes=list(scratch),
+        cost_estimate=cost,
         compiler_params=pltpu.CompilerParams(vmem_limit_bytes=12 * 2**20),
     )(*operands)
 
 
 def kept(x):
     return pltpu.with_memory_space_constraint(x, pltpu.VMEM)
+
+
+def far(x):
+    return pltpu.with_memory_space_constraint(x, pltpu.HBM)
 
 
 def local(states, terrain, depth_table, spread_table, mixing):
@@ -318,46 +378,68 @@
     forth = [(i, i + 1) for i in range(strips - 1)]
     back = [(j, i) for i, j in forth]
 
-    chunks = pl.pallas_call(
-        pack_kernel,
-        out_shape=pltpu.VMEM((S, NALL, 8, L), F32),
-        in_specs=[pl.BlockSpec(memory_space=pltpu.HBM)],
+    def to_chunks(value):
+        return lax.all_to_all(value, "sub", split_axis=0, concat_axis=0, tiled=True)
+
+    hbm = pl.BlockSpec(memory_space=pltpu.HBM)
+    limit = pltpu.CompilerParams(vmem_limit_bytes=12 * 2**20)
+    outer = pl.pallas_call(
+        outer_kernel,
+        out_shape=pltpu.VMEM((S, NOUTER, 8, L), F32),
+        in_specs=[SMEM, hbm, hbm],
         out_specs=VMEM,
         scratch_shapes=[
-            pltpu.VMEM((F, rows, S * L), F32),
-            pltpu.SemaphoreType.DMA((F, G)),
+            pltpu.VMEM((F, G, 8, S * L), F32),
+            pltpu.VMEM((16, S * L), jnp.int32),
+            pltpu.VMEM((2, 8, S * L), F32),
+            pltpu.SemaphoreType.DMA((9,)),
         ],
-        compiler_params=pltpu.CompilerParams(vmem_limit_bytes=12 * 2**20),
-    )(pltpu.with_memory_space_constraint(states[0], pltpu.HBM))
-    held = lax.all_to_all(chunks, "sub", split_axis=0, concat_axis=0, tiled=True)
-
-    edge = pltpu.VMEM((2, 8, L), jnp.int32)
-    up, down = kernel(terrain_kernel, (edge, edge), (place, terrain), 1)
-    terrain_above = lax.ppermute(down, "tile", forth)
-    terrain_below = lax.ppermute(up, "tile", back)
+        compiler_params=limit,
+    )(far(depth_table), far(states[0]), far(terrain))
+    outer = to_chunks(outer)
+    halo = pltpu.VMEM((NHALO, 8, L), F32)
+    up, down = kernel(edge_kernel, (halo, halo), (place, kept(outer), terrain), 1)
+    above = lax.ppermute(down, "tile", forth)
+    below = lax.ppermute(up, "tile", back)
+    inner = pl.pallas_call(
+        inner_kernel,
+        out_shape=pltpu.VMEM((S, NINNER, 8, L), F32),
+        in_specs=[hbm],
+        out_specs=VMEM,
+        scratch_shapes=[
+            pltpu.VMEM((F, G, 8, S * L), F32),
+            pltpu.VMEM((8, S * L), F32),
+            pltpu.SemaphoreType.DMA((8,)),
+        ],
+        compiler_params=limit,
+    )(far(states[0]))
+    anywhere = pl.BlockSpec(memory_space=pl.ANY)
+    inner = pl.pallas_call(
+        follow_kernel,
+        out_shape=jax.ShapeDtypeStruct(inner.shape, F32),
+        in_specs=[anywhere, anywhere],
+        out_specs=anywhere,
+        input_output_aliases={0: 0},
+    )(inner, up)
+    inner = to_chunks(inner)
     coef = kernel(
         coef_kernel,
         pltpu.VMEM((2, DEPTH, TALL, L), F32),
-        (place, depth_table, spread_table, terrain, kept(terrain_above), kept(terrain_below)),
+        (place, depth_table, spread_table, terrain, kept(above), kept(below)),
         3,
         [pltpu.VMEM((3, 8 * (G + 2), L), F32)],
+        cost=pl.CostEstimate(flops=10**11, bytes_accessed=10**6, transcendentals=0),
     )
     weights = jnp.kron(jnp.eye(BLOCKS, dtype=F32), mixing)
-
-    halo = pltpu.VMEM((NHALO, 8, L), F32)
-    up, down = kernel(
-        edge_kernel, (halo, halo), (place, depth_table, kept(held), terrain), 2
-    )
-    above = lax.ppermute(down, "tile", forth)
-    below = lax.ppermute(up, "tile", back)
 
     plane = (DEPTH, TALL, L)
     mixed = kernel(
         main_kernel,
-        pltpu.VMEM((S * NMAIN * 8, L), F32),
+        pltpu.VMEM((S * F * rows, L), F32),
         (
             place,
-            kept(held.reshape(S * NALL * 8, L)),
+            kept(outer.reshape(S * NOUTER * 8, L)),
+            kept(inner.reshape(S * NINNER * 8, L)),
             kept(above.reshape(NHALO * 8, L)),
             kept(below.reshape(NHALO * 8, L)),
             kept(coef),

time: 70 us -> 68.7 us (0.981)
  the two profiles are of different devices: /device:TPU:249 before, /device:TPU:256 now
where the time goes in v4:
time: 68.7 us; the launch traced here: 68.3 us
  waiting for transfers between devices  20 us (29%)
  starting transfers between devices  19.1 us (28%)
  blocking collectives  16.3 us (24%)
  Pallas kernels  11.6 us (17%)
  local copies, waits for them, and re-layouts  1 us (1%)
    all_to_all x1, blocking collectives, local(): lax.all_to_all(mixed.reshape(S, F, rows, L), 'sub', split_axis=0, concat_...  16.3 us
    all_to_all x2, waiting for transfers between devices, to_chunks(): return lax.all_to_all(value, 'sub', split_axis=0, concat_axis=0, tiled=True)  14.7 us
    all_to_all x2, starting transfers between devices, to_chunks(): return lax.all_to_all(value, 'sub', split_axis=0, concat_axis=0, tiled=True)  9.01 us
    pallas_call x4, Pallas kernels, kernel(): pl.pallas_call(body, out_shape=out, in_specs=specs, out_specs=(out_specs,...  7.38 us
    ppermute x1, starting transfers between devices, local(): below = lax.ppermute(up, 'tile', back)  5.56 us
    ppermute x1, waiting for transfers between devices, local(): above = lax.ppermute(down, 'tile', forth)  4.82 us
    ppermute x1, starting transfers between devices, local(): above = lax.ppermute(down, 'tile', forth)  4.5 us
    pallas_call x1, Pallas kernels, local(): pl.pallas_call(outer_kernel, out_shape=pltpu.VMEM((S, NOUTER, 8, L), F32)...  2.82 us
  transfers between devices with their start and end apart: 4, of which 4 were waited for; matrix products, arithmetic and copies ran while one was open for 1% of the time, Pallas kernels for 4%

profile of v4, /device:TPU:256, one launch (start us, length us, event | category | flops | bytes accessed | tf_op | source)
XLA Modules:
  0.0 68.3 jit_solution(7433689565953063238)
XLA Ops:
  0.0 2.8 %shard_map.55 = f32[16,7,8,128]{3,2,1,0:T(8,128)} custom-call(f32[8]{0:T(128)} %depth_ref.3, f32[3,32,2048]{2,1,0:T(8,128)} %bitcast.16, s32[32,2048]{1,0:T(8,128)} %ter_ref.3), custom_call_target="tpu_custom_call" | custom-call | tf_op jit(solution)/shard_map/pallas_call | solution.py:386
  2.8 5.4 %all-to-all-start = ((f32[16,7,8,128]{3,2,1,0:T(8,128)}), f32[16,7,8,128]{3,2,1,0:T(8,128)S(1)}, u32[]{:S(2)}, u32[]{:S(2)}) async-start(f32[16,7,8,128]{3,2,1,0:T(8,128)} %shard_map.55), calls=%async_computation | async-start | bytes 917504 | tf_op jit(solution)/shard_map/all_to_all | solution.py:382
  8.3 0.0 copy-start.1
  8.3 1.4 %shard_map.56.x_ref = f32[16,8,8,128]{3,2,1,0:T(8,128)S(1)} custom-call(f32[3,32,2048]{2,1,0:T(8,128)} %bitcast.17), custom_call_target="tpu_custom_call" | custom-call | tf_op jit(solution)/shard_map/pallas_call | solution.py:404
  9.7 0.0 copy-start
  9.7 0.8 %copy-done = f32[16,8,8,128]{3,2,1,0:T(8,128)} copy-done((f32[16,8,8,128]{3,2,1,0:T(8,128)}, f32[16,8,8,128]{3,2,1,0:T(8,128)S(1)}, u32[]{:S(2)}) %copy-start) | copy-done | bytes 524312
  10.5 0.1 pad_add_fusion.place_ref
  10.6 7.9 %all-to-all-done.outer_ref = f32[16,7,8,128]{3,2,1,0:T(8,128)S(1)} async-done(((f32[16,7,8,128]{3,2,1,0:T(8,128)}), f32[16,7,8,128]{3,2,1,0:T(8,128)S(1)}, u32[]{:S(2)}, u32[]{:S(2)}) %all-to-all-start) | async-done | bytes 458784 | tf_op jit(solution)/shard_map/all_to_all | solution.py:382
  18.4 0.0 copy-done.1
  18.4 0.0 copy-start.5
  18.4 0.6 shard_map.57
  19.1 0.0 copy-start.2
  19.1 4.5 %collective-permute-start = (f32[57,8,128]{2,1,0:T(8,128)S(1)}, f32[57,8,128]{2,1,0:T(8,128)S(1)}, u32[]{:S(2)}, u32[]{:S(2)}) collective-permute-start(f32[57,8,128]{2,1,0:T(8,128)S(1)} %get-tuple-element.8), channel_id=1, source_target_pairs={{0,1},{1,2},{2,3},{3,4},{4,5},{5,6},{6,7},{7,8},{8,9},{9,10},{10,1... | collective-permute-start | bytes 700424 | tf_op jit(solution)/shard_map/ppermute | solution.py:402
  23.6 5.6 %collective-permute-start.1 = (f32[57,8,128]{2,1,0:T(8,128)S(1)}, f32[57,8,128]{2,1,0:T(8,128)S(1)}, u32[]{:S(2)}, u32[]{:S(2)}) collective-permute-start(f32[57,8,128]{2,1,0:T(8,128)S(1)} %get-tuple-element.7.after_ref), channel_id=1, source_target_pairs={{1,0},{2,1},{3,2},{4,3},{5,4},{6,5},{7,6},{8,7},{9,8},{10,9},{11,1... | collective-permute-start | bytes 700424 | tf_op jit(solution)/shard_map/ppermute | solution.py:403
  29.1 0.0 copy-done.5
  29.2 0.1 broadcast_multiply_fusion
  29.3 0.0 copy-done.2
  29.3 0.2 mul.31.weights_ref
  29.5 0.0 copy-start.3
  29.5 0.0 copy-start.4
  29.5 3.6 %all-to-all-start.1 = ((f32[16,8,8,128]{3,2,1,0:T(8,128)}), f32[16,8,8,128]{3,2,1,0:T(8,128)S(1)}, u32[]{:S(2)}, u32[]{:S(2)}) async-start(f32[16,8,8,128]{3,2,1,0:T(8,128)} %shard_map.58), calls=%async_computation.1 | async-start | bytes 1048576 | tf_op jit(solution)/shard_map/all_to_all | solution.py:382
  33.1 4.8 %collective-permute-done.above_ref = f32[57,8,128]{2,1,0:T(8,128)S(1)} collective-permute-done((f32[57,8,128]{2,1,0:T(8,128)S(1)}, f32[57,8,128]{2,1,0:T(8,128)S(1)}, u32[]{:S(2)}, u32[]{:S(2)}) %collective-permute-start) | collective-permute-done | bytes 233504 | tf_op jit(solution)/shard_map/ppermute | solution.py:402
  37.9 0.5 collective-permute-done.1.below_ref
  38.4 0.0 copy-done.3
  38.4 0.0 copy-done.4
  38.4 1.0 %shard_map.59.coef_ref = f32[2,6,160,128]{3,2,1,0:T(8,128)S(1)} custom-call(s32[3]{0:T(128)S(1)} %pad_add_fusion.place_ref, f32[8]{0:T(128)S(1)} %copy-done.3, f32[8]{0:T(128)S(1)} %copy-done.4, s32[32,2048]{1,0:T(8,128)S(1)} %copy-done.1, f32[57,8,128]{2,1,0:T(8,128)S(1)} %collective-permute-done.above_ref, f32[57,8,128]{2,1,0:T(8,128)S(1)} %collective-permute-done.1.below_ref), custom_call_target="tpu_custom_call" | custom-call | flops 99999997952 | bytes 1000000 | tf_op jit(solution)/shard_map/pallas_call | solution.py:353
  39.4 6.8 %all-to-all-done.1 = f32[16,8,8,128]{3,2,1,0:T(8,128)S(1)} async-done(((f32[16,8,8,128]{3,2,1,0:T(8,128)}), f32[16,8,8,128]{3,2,1,0:T(8,128)S(1)}, u32[]{:S(2)}, u32[]{:S(2)}) %all-to-all-start.1) | async-done | bytes 524320 | tf_op jit(solution)/shard_map/all_to_all | solution.py:382
  46.3 4.7 %shard_map.60 = f32[1536,128]{1,0:T(8,128)S(1)} custom-call(s32[3]{0:T(128)S(1)} %pad_add_fusion.place_ref, f32[896,128]{1,0:T(8,128)S(1)} %bitcast.11, f32[1024,128]{1,0:T(8,128)S(1)} %bitcast.13, f32[456,128]{1,0:T(8,128)S(1)} %bitcast.14, f32[456,128]{1,0:T(8,128)S(1)} %bitcast.15, f32[2,6,160,128]{3,2,1,0:T(8,128)S(1)} %shard_map.59.coef_ref, ...), custom_call_target="tpu_custom_call" | custom-call | tf_op jit(solution)/shard_map/pallas_call | solution.py:353
  51.0 16.3 %all_to_all.15.x_ref = f32[16,3,32,128]{3,2,1,0:T(8,128)S(1)} all-to-all(f32[16,3,32,128]{3,2,1,0:T(8,128)S(1)} %bitcast.12), channel_id=1, replica_groups=mesh['sub'=16,'tile'=32] {'sub'}, dimensions={0} | all-to-all | bytes 1572864 | tf_op jit(solution)/shard_map/all_to_all | solution.py:456
  67.3 1.0 %shard_map.61 = f32[3,32,2048]{2,1,0:T(8,128)} custom-call(f32[16,3,32,128]{3,2,1,0:T(8,128)S(1)} %all_to_all.15.x_ref), custom_call_target="tpu_custom_call" | custom-call | tf_op jit(solution)/shard_map/pallas_call | solution.py:353
  (2 shorter events, 0.0 us)
Async XLA Ops:
  2.8 15.6 %all-to-all-start = ((f32[16,7,8,128]{3,2,1,0:T(8,128)}), f32[16,7,8,128]{3,2,1,0:T(8,128)S(1)}, u32[]{:S(2)}, u32[]{:S(2)}) async-start(f32[16,7,8,128]{3,2,1,0:T(8,128)} %shard_map.55), calls=%async_computation | async-start | bytes 917504 | tf_op jit(solution)/shard_map/all_to_all | solution.py:382
  8.3 10.2 %copy-start.1 = (s32[32,2048]{1,0:T(8,128)S(1)}, s32[32,2048]{1,0:T(8,128)}, u32[]{:S(2)}) copy-start(s32[32,2048]{1,0:T(8,128)} %ter_ref.3) | copy-start | bytes 786436
  9.7 0.8 %copy-start = (f32[16,8,8,128]{3,2,1,0:T(8,128)}, f32[16,8,8,128]{3,2,1,0:T(8,128)S(1)}, u32[]{:S(2)}) copy-start(f32[16,8,8,128]{3,2,1,0:T(8,128)S(1)} %shard_map.56.x_ref) | copy-start | bytes 1572868
  18.4 10.7 %copy-start.5 = (f32[16,16]{1,0:T(8,128)S(1)}, f32[16,16]{1,0:T(8,128)}, u32[]{:S(2)}) copy-start(f32[16,16]{1,0:T(8,128)} %param.9) | copy-start | bytes 3076
  19.1 10.2 %copy-start.2 = (f32[57,8,128]{2,1,0:T(8,128)}, f32[57,8,128]{2,1,0:T(8,128)S(1)}, u32[]{:S(2)}) copy-start(f32[57,8,128]{2,1,0:T(8,128)S(1)} %get-tuple-element.7.after_ref) | copy-start | bytes 700420
  19.1 18.9 %collective-permute-start = (f32[57,8,128]{2,1,0:T(8,128)S(1)}, f32[57,8,128]{2,1,0:T(8,128)S(1)}, u32[]{:S(2)}, u32[]{:S(2)}) collective-permute-start(f32[57,8,128]{2,1,0:T(8,128)S(1)} %get-tuple-element.8), channel_id=1, source_target_pairs={{0,1},{1,2},{2,3},{3,4},{4,5},{5,6},{6,7},{7,8},{8,9},{9,10},{10,1... | collective-permute-start | bytes 700424 | tf_op jit(solution)/shard_map/ppermute | solution.py:402
  23.6 14.8 %collective-permute-start.1 = (f32[57,8,128]{2,1,0:T(8,128)S(1)}, f32[57,8,128]{2,1,0:T(8,128)S(1)}, u32[]{:S(2)}, u32[]{:S(2)}) collective-permute-start(f32[57,8,128]{2,1,0:T(8,128)S(1)} %get-tuple-element.7.after_ref), channel_id=1, source_target_pairs={{1,0},{2,1},{3,2},{4,3},{5,4},{6,5},{7,6},{8,7},{9,8},{10,9},{11,1... | collective-permute-start | bytes 700424 | tf_op jit(solution)/shard_map/ppermute | solution.py:403
  29.5 8.9 %copy-start.3 = (f32[8]{0:T(128)S(1)}, f32[8]{0:T(128)}, u32[]{:S(2)}) copy-start(f32[8]{0:T(128)} %depth_ref.3) | copy-start | bytes 100
  29.5 8.9 %copy-start.4 = (f32[8]{0:T(128)S(1)}, f32[8]{0:T(128)}, u32[]{:S(2)}) copy-start(f32[8]{0:T(128)} %spread_ref.1) | copy-start | bytes 100
  29.5 16.8 %all-to-all-start.1 = ((f32[16,8,8,128]{3,2,1,0:T(8,128)}), f32[16,8,8,128]{3,2,1,0:T(8,128)S(1)}, u32[]{:S(2)}, u32[]{:S(2)}) async-start(f32[16,8,8,128]{3,2,1,0:T(8,128)} %shard_map.58), calls=%async_computation.1 | async-start | bytes 1048576 | tf_op jit(solution)/shard_map/all_to_all | solution.py:382

commit v5 on v4

--- a/solution.py
+++ b/solution.py
@@ -14,8 +14,7 @@
 R = 8
 C = 9
 W = 2 * C
-NOUTER = 2 * F + 1
-NINNER = 2 * F + 2
+NPART = 2 * F + 1
 NHALO = S * F + S // 2 + 1
 SPARE = 2 * F * W
 BLOCKS = 8
@@ -48,7 +47,7 @@
         copy.wait()
 
 
-def pack(o_ref, tile, packed_of):
+def pack(o_ref, tile):
     lane = iota(1)
 
     def sides(q, c, at):
@@ -56,7 +55,7 @@
         return pltpu.roll(value, at + C, 1)
 
     for c in range(S):
-        packed = packed_of(c, sides)
+        packed = jnp.zeros((8, L), F32)
         for q in reversed(range(2 * F)):
             o_ref[c, q] = tile(q, c)
             packed = jnp.where(lane < W * q + W, sides(q, c, W * q), packed)
@@ -84,26 +83,17 @@
             return rows_s[q // F, :, cols]
         return x_s[q % F, q // F * (G - 1), :, cols]
 
-    pack(o_ref, tile, lambda c, sides: jnp.zeros((8, L), F32))
-
-
-def inner_kernel(x_hbm, o_ref, x_s, rows_s, sems):
-    row = iota(0, (8, S * L))
-    groups = [(0, 0), (0, 3)] + [(f, g) for f in range(F) for g in (1, 2)]
-    fetch([(x_hbm.at[f, pl.ds(8 * g, 8)], x_s.at[f, g]) for f, g in groups], sems)
-    rows_s[...] = jnp.where(row == 0, pltpu.roll(x_s[0, 0], 1, 0), pltpu.roll(x_s[0, 3], 1, 0))
+    pack(o_ref, tile)
+
+
+def inner_kernel(x_hbm, o_ref, x_s, sems):
+    groups = [(f, g) for f in range(F) for g in range(2)]
+    fetch([(x_hbm.at[f, pl.ds(8 * g + 8, 8)], x_s.at[f, g]) for f, g in groups], sems)
 
     def tile(q, c):
-        cols = slice(L * c, L * c + L)
-        if q == 2 * F:
-            return rows_s[:, cols]
-        return x_s[q % F, 1 + q // F, :, cols]
-
-    def packed_of(c, sides):
-        o_ref[c, 2 * F + 1] = tile(2 * F, c)
-        return sides(2 * F, c, SPARE)
-
-    pack(o_ref, tile, packed_of)
+        return x_s[q % F, q // F, :, L * c : L * c + L]
+
+    pack(o_ref, tile)
 
 
 def follow_kernel(x_ref, after_ref, o_ref):
@@ -205,18 +195,16 @@
         slope_s[r] = -0.25 * inside_of(first, total, r, (PART, L))
 
     def outer_rows(at):
-        return outer_ref[pl.ds(at, S, 8 * NOUTER), :]
+        return outer_ref[pl.ds(at, S, 8 * NPART), :]
 
     def inner_rows(at):
-        return inner_ref[pl.ds(at, S, 8 * NINNER), :]
+        return inner_ref[pl.ds(at, S, 8 * NPART), :]
 
     def main_rows(f, row):
         if row < 0:
             return above_ref[pl.ds(8 * f + row + R, S, 8 * F), :]
         if row >= 8 * G:
             return below_ref[pl.ds(8 * f + row - 8 * G, S, 8 * F), :]
-        if f == 0 and row in (7, 24):
-            return inner_rows(8 * 7 + row // 8 // 3)
         if 8 <= row < 24:
             return inner_rows(8 * ((row // 8 - 1) * F + f) + row % 8)
         return outer_rows(8 * (row // 24 * F + f) + row % 8)
@@ -233,12 +221,7 @@
             value = inner_rows(8 * 6 + row % 8)
             return turned(value, 3 * W) if row >= 16 else value
         value = outer_rows(8 * 6 + row % 8)
-        if row >= 24:
-            value = turned(value, 3 * W)
-        if row in (7, 24):
-            height = turned(inner_rows(8 * 6 + row // 8 // 3), SPARE)
-            value = jnp.where(lane < W, height, value)
-        return value
+        return turned(value, 3 * W) if row >= 24 else value
 
     for r in range(DEPTH):
         for f in range(F):
@@ -249,6 +232,12 @@
         for f in range(F):
             a_s[f, r, EDGE - C : EDGE, :] = sides[W * f : W * f + C]
             a_s[f, r, EDGE + L : EDGE + L + C, :] = sides[W * f + C : W * f + W]
+
+    block = lax.div(iota(1, (TALL, L)), S)
+    for row, beyond, sign in ((7, 8, 0.25), (24, 23, -0.25)):
+        (at_block, r), flux_r = divmod(row + R, DEPTH), (beyond + R) % DEPTH
+        flux = sign * coef_ref[0, flux_r] * a_s[1, flux_r]
+        a_s[0, r] = a_s[0, r] + jnp.where(block == at_block, flux, 0.0)
 
     parts = [8 + PART * i for i in range((TALL - 16) // PART)]
 
@@ -385,7 +374,7 @@
     limit = pltpu.CompilerParams(vmem_limit_bytes=12 * 2**20)
     outer = pl.pallas_call(
         outer_kernel,
-        out_shape=pltpu.VMEM((S, NOUTER, 8, L), F32),
+        out_shape=pltpu.VMEM((S, NPART, 8, L), F32),
         in_specs=[SMEM, hbm, hbm],
         out_specs=VMEM,
         scratch_shapes=[
@@ -403,13 +392,12 @@
     below = lax.ppermute(up, "tile", back)
     inner = pl.pallas_call(
         inner_kernel,
-        out_shape=pltpu.VMEM((S, NINNER, 8, L), F32),
+        out_shape=pltpu.VMEM((S, NPART, 8, L), F32),
         in_specs=[hbm],
         out_specs=VMEM,
         scratch_shapes=[
-            pltpu.VMEM((F, G, 8, S * L), F32),
-            pltpu.VMEM((8, S * L), F32),
-            pltpu.SemaphoreType.DMA((8,)),
+            pltpu.VMEM((F, 2, 8, S * L), F32),
+            pltpu.SemaphoreType.DMA((2 * F,)),
         ],
         compiler_params=limit,
     )(far(states[0]))
@@ -438,8 +426,8 @@
         pltpu.VMEM((S * F * rows, L), F32),
         (
             place,
-            kept(outer.reshape(S * NOUTER * 8, L)),
-            kept(inner.reshape(S * NINNER * 8, L)),
+            kept(outer.reshape(S * NPART * 8, L)),
+            kept(inner.reshape(S * NPART * 8, L)),
             kept(above.reshape(NHALO * 8, L)),
             kept(below.reshape(NHALO * 8, L)),
             kept(coef),

time: 68.7 us -> 68 us (0.990)
  transfers between devices with their start and end apart: 4 -> 4, of which waited for: 4 -> 4; matrix products, arithmetic and copies ran while one was open for 1% -> 1% of each run, Pallas kernels for 4% -> 3%
where the time goes in v5:
time: 68 us; the launch traced here: 67.6 us
  waiting for transfers between devices  19.4 us (29%)
  starting transfers between devices  19.1 us (28%)
  blocking collectives  16.3 us (24%)
  Pallas kernels  11.5 us (17%)
  local copies, waits for them, and re-layouts  0.99 us (1%)
    all_to_all x1, blocking collectives, local(): lax.all_to_all(mixed.reshape(S, F, rows, L), 'sub', split_axis=0, concat_...  16.3 us
    all_to_all x2, waiting for transfers between devices, to_chunks(): return lax.all_to_all(value, 'sub', split_axis=0, concat_axis=0, tiled=True)  14.1 us
    all_to_all x2, starting transfers between devices, to_chunks(): return lax.all_to_all(value, 'sub', split_axis=0, concat_axis=0, tiled=True)  9 us
    pallas_call x4, Pallas kernels, kernel(): pl.pallas_call(body, out_shape=out, in_specs=specs, out_specs=(out_specs,...  7.42 us
    ppermute x1, starting transfers between devices, local(): below = lax.ppermute(up, 'tile', back)  5.56 us
    ppermute x1, waiting for transfers between devices, local(): above = lax.ppermute(down, 'tile', forth)  4.84 us
    ppermute x1, starting transfers between devices, local(): above = lax.ppermute(down, 'tile', forth)  4.5 us
    pallas_call x1, Pallas kernels, local(): pl.pallas_call(outer_kernel, out_shape=pltpu.VMEM((S, NPART, 8, L), F32),...  2.8 us
  transfers between devices with their start and end apart: 4, of which 4 were waited for; matrix products, arithmetic and copies ran while one was open for 1% of the time, Pallas kernels for 3%

profile of v5, /device:TPU:256, one launch (start us, length us, event | category | flops | bytes accessed | tf_op | source)
XLA Modules:
  0.0 67.6 jit_solution(1559237838467994912)
XLA Ops:
  0.0 2.8 %shard_map.55 = f32[16,7,8,128]{3,2,1,0:T(8,128)} custom-call(f32[8]{0:T(128)} %depth_ref.3, f32[3,32,2048]{2,1,0:T(8,128)} %bitcast.16, s32[32,2048]{1,0:T(8,128)} %ter_ref.3), custom_call_target="tpu_custom_call" | custom-call | tf_op jit(solution)/shard_map/pallas_call | solution.py:375
  2.8 5.4 %all-to-all-start = ((f32[16,7,8,128]{3,2,1,0:T(8,128)}), f32[16,7,8,128]{3,2,1,0:T(8,128)S(1)}, u32[]{:S(2)}, u32[]{:S(2)}) async-start(f32[16,7,8,128]{3,2,1,0:T(8,128)} %shard_map.55), calls=%async_computation | async-start | bytes 917504 | tf_op jit(solution)/shard_map/all_to_all | solution.py:371
  8.2 0.0 copy-start.1
  8.3 1.3 %shard_map.56.x_ref = f32[16,7,8,128]{3,2,1,0:T(8,128)S(1)} custom-call(f32[3,32,2048]{2,1,0:T(8,128)} %bitcast.17), custom_call_target="tpu_custom_call" | custom-call | tf_op jit(solution)/shard_map/pallas_call | solution.py:393
  9.6 0.0 copy-start
  9.6 0.8 %copy-done = f32[16,7,8,128]{3,2,1,0:T(8,128)} copy-done((f32[16,7,8,128]{3,2,1,0:T(8,128)}, f32[16,7,8,128]{3,2,1,0:T(8,128)S(1)}, u32[]{:S(2)}) %copy-start) | copy-done | bytes 458776
  10.4 0.1 pad_add_fusion.place_ref
  10.4 8.0 %all-to-all-done.outer_ref = f32[16,7,8,128]{3,2,1,0:T(8,128)S(1)} async-done(((f32[16,7,8,128]{3,2,1,0:T(8,128)}), f32[16,7,8,128]{3,2,1,0:T(8,128)S(1)}, u32[]{:S(2)}, u32[]{:S(2)}) %all-to-all-start) | async-done | bytes 458784 | tf_op jit(solution)/shard_map/all_to_all | solution.py:371
  18.4 0.0 copy-done.1
  18.4 0.0 copy-start.5
  18.4 0.6 shard_map.57
  19.0 0.0 copy-start.2
  19.1 4.5 %collective-permute-start = (f32[57,8,128]{2,1,0:T(8,128)S(1)}, f32[57,8,128]{2,1,0:T(8,128)S(1)}, u32[]{:S(2)}, u32[]{:S(2)}) collective-permute-start(f32[57,8,128]{2,1,0:T(8,128)S(1)} %get-tuple-element.8), channel_id=1, source_target_pairs={{0,1},{1,2},{2,3},{3,4},{4,5},{5,6},{6,7},{7,8},{8,9},{9,10},{10,1... | collective-permute-start | bytes 700424 | tf_op jit(solution)/shard_map/ppermute | solution.py:391
  23.6 5.6 %collective-permute-start.1 = (f32[57,8,128]{2,1,0:T(8,128)S(1)}, f32[57,8,128]{2,1,0:T(8,128)S(1)}, u32[]{:S(2)}, u32[]{:S(2)}) collective-permute-start(f32[57,8,128]{2,1,0:T(8,128)S(1)} %get-tuple-element.7.after_ref), channel_id=1, source_target_pairs={{1,0},{2,1},{3,2},{4,3},{5,4},{6,5},{7,6},{8,7},{9,8},{10,9},{11,1... | collective-permute-start | bytes 700424 | tf_op jit(solution)/shard_map/ppermute | solution.py:392
  29.1 0.0 copy-done.5
  29.1 0.1 broadcast_multiply_fusion
  29.2 0.0 copy-done.2
  29.3 0.2 mul.31.weights_ref
  29.5 0.0 copy-start.3
  29.5 0.0 copy-start.4
  29.5 3.6 %all-to-all-start.1 = ((f32[16,7,8,128]{3,2,1,0:T(8,128)}), f32[16,7,8,128]{3,2,1,0:T(8,128)S(1)}, u32[]{:S(2)}, u32[]{:S(2)}) async-start(f32[16,7,8,128]{3,2,1,0:T(8,128)} %shard_map.58), calls=%async_computation.1 | async-start | bytes 917504 | tf_op jit(solution)/shard_map/all_to_all | solution.py:371
  33.1 4.8 %collective-permute-done.above_ref = f32[57,8,128]{2,1,0:T(8,128)S(1)} collective-permute-done((f32[57,8,128]{2,1,0:T(8,128)S(1)}, f32[57,8,128]{2,1,0:T(8,128)S(1)}, u32[]{:S(2)}, u32[]{:S(2)}) %collective-permute-start) | collective-permute-done | bytes 233504 | tf_op jit(solution)/shard_map/ppermute | solution.py:391
  37.9 0.5 collective-permute-done.1.below_ref
  38.4 0.0 copy-done.3
  38.4 0.0 copy-done.4
  38.4 1.0 %shard_map.59.coef_ref = f32[2,6,160,128]{3,2,1,0:T(8,128)S(1)} custom-call(s32[3]{0:T(128)S(1)} %pad_add_fusion.place_ref, f32[8]{0:T(128)S(1)} %copy-done.3, f32[8]{0:T(128)S(1)} %copy-done.4, s32[32,2048]{1,0:T(8,128)S(1)} %copy-done.1, f32[57,8,128]{2,1,0:T(8,128)S(1)} %collective-permute-done.above_ref, f32[57,8,128]{2,1,0:T(8,128)S(1)} %collective-permute-done.1.below_ref), custom_call_target="tpu_custom_call" | custom-call | flops 99999997952 | bytes 1000000 | tf_op jit(solution)/shard_map/pallas_call | solution.py:342
  39.4 6.1 %all-to-all-done.1 = f32[16,7,8,128]{3,2,1,0:T(8,128)S(1)} async-done(((f32[16,7,8,128]{3,2,1,0:T(8,128)}), f32[16,7,8,128]{3,2,1,0:T(8,128)S(1)}, u32[]{:S(2)}, u32[]{:S(2)}) %all-to-all-start.1) | async-done | bytes 458784 | tf_op jit(solution)/shard_map/all_to_all | solution.py:371
  45.5 4.8 %shard_map.60 = f32[1536,128]{1,0:T(8,128)S(1)} custom-call(s32[3]{0:T(128)S(1)} %pad_add_fusion.place_ref, f32[896,128]{1,0:T(8,128)S(1)} %bitcast.11, f32[896,128]{1,0:T(8,128)S(1)} %bitcast.13, f32[456,128]{1,0:T(8,128)S(1)} %bitcast.14, f32[456,128]{1,0:T(8,128)S(1)} %bitcast.15, f32[2,6,160,128]{3,2,1,0:T(8,128)S(1)} %shard_map.59.coef_ref, ...), custom_call_target="tpu_custom_call" | custom-call | tf_op jit(solution)/shard_map/pallas_call | solution.py:342
  50.3 16.3 %all_to_all.15.x_ref = f32[16,3,32,128]{3,2,1,0:T(8,128)S(1)} all-to-all(f32[16,3,32,128]{3,2,1,0:T(8,128)S(1)} %bitcast.12), channel_id=1, replica_groups=mesh['sub'=16,'tile'=32] {'sub'}, dimensions={0} | all-to-all | bytes 1572864 | tf_op jit(solution)/shard_map/all_to_all | solution.py:444
  66.6 1.0 %shard_map.61 = f32[3,32,2048]{2,1,0:T(8,128)} custom-call(f32[16,3,32,128]{3,2,1,0:T(8,128)S(1)} %all_to_all.15.x_ref), custom_call_target="tpu_custom_call" | custom-call | tf_op jit(solution)/shard_map/pallas_call | solution.py:342
  (2 shorter events, 0.0 us)
Async XLA Ops:
  2.8 15.6 %all-to-all-start = ((f32[16,7,8,128]{3,2,1,0:T(8,128)}), f32[16,7,8,128]{3,2,1,0:T(8,128)S(1)}, u32[]{:S(2)}, u32[]{:S(2)}) async-start(f32[16,7,8,128]{3,2,1,0:T(8,128)} %shard_map.55), calls=%async_computation | async-start | bytes 917504 | tf_op jit(solution)/shard_map/all_to_all | solution.py:371
  8.2 10.2 %copy-start.1 = (s32[32,2048]{1,0:T(8,128)S(1)}, s32[32,2048]{1,0:T(8,128)}, u32[]{:S(2)}) copy-start(s32[32,2048]{1,0:T(8,128)} %ter_ref.3) | copy-start | bytes 786436
  9.6 0.8 %copy-start = (f32[16,7,8,128]{3,2,1,0:T(8,128)}, f32[16,7,8,128]{3,2,1,0:T(8,128)S(1)}, u32[]{:S(2)}) copy-start(f32[16,7,8,128]{3,2,1,0:T(8,128)S(1)} %shard_map.56.x_ref) | copy-start | bytes 1376260
  18.4 10.7 %copy-start.5 = (f32[16,16]{1,0:T(8,128)S(1)}, f32[16,16]{1,0:T(8,128)}, u32[]{:S(2)}) copy-start(f32[16,16]{1,0:T(8,128)} %param.9) | copy-start | bytes 3076
  19.0 10.2 %copy-start.2 = (f32[57,8,128]{2,1,0:T(8,128)}, f32[57,8,128]{2,1,0:T(8,128)S(1)}, u32[]{:S(2)}) copy-start(f32[57,8,128]{2,1,0:T(8,128)S(1)} %get-tuple-element.7.after_ref) | copy-start | bytes 700420
  19.1 18.9 %collective-permute-start = (f32[57,8,128]{2,1,0:T(8,128)S(1)}, f32[57,8,128]{2,1,0:T(8,128)S(1)}, u32[]{:S(2)}, u32[]{:S(2)}) collective-permute-start(f32[57,8,128]{2,1,0:T(8,128)S(1)} %get-tuple-element.8), channel_id=1, source_target_pairs={{0,1},{1,2},{2,3},{3,4},{4,5},{5,6},{6,7},{7,8},{8,9},{9,10},{10,1... | collective-permute-start | bytes 700424 | tf_op jit(solution)/shard_map/ppermute | solution.py:391
  23.6 14.8 %collective-permute-start.1 = (f32[57,8,128]{2,1,0:T(8,128)S(1)}, f32[57,8,128]{2,1,0:T(8,128)S(1)}, u32[]{:S(2)}, u32[]{:S(2)}) collective-permute-start(f32[57,8,128]{2,1,0:T(8,128)S(1)} %get-tuple-element.7.after_ref), channel_id=1, source_target_pairs={{1,0},{2,1},{3,2},{4,3},{5,4},{6,5},{7,6},{8,7},{9,8},{10,9},{11,1... | collective-permute-start | bytes 700424 | tf_op jit(solution)/shard_map/ppermute | solution.py:392
  29.5 8.9 %copy-start.3 = (f32[8]{0:T(128)S(1)}, f32[8]{0:T(128)}, u32[]{:S(2)}) copy-start(f32[8]{0:T(128)} %depth_ref.3) | copy-start | bytes 100
  29.5 8.9 %copy-start.4 = (f32[8]{0:T(128)S(1)}, f32[8]{0:T(128)}, u32[]{:S(2)}) copy-start(f32[8]{0:T(128)} %spread_ref.1) | copy-start | bytes 100
  29.5 16.1 %all-to-all-start.1 = ((f32[16,7,8,128]{3,2,1,0:T(8,128)}), f32[16,7,8,128]{3,2,1,0:T(8,128)S(1)}, u32[]{:S(2)}, u32[]{:S(2)}) async-start(f32[16,7,8,128]{3,2,1,0:T(8,128)} %shard_map.58), calls=%async_computation.1 | async-start | bytes 917504 | tf_op jit(solution)/shard_map/all_to_all | solution.py:371

commit v6 on v5

--- a/solution.py
+++ b/solution.py
@@ -43,6 +43,10 @@
     copies = [pltpu.make_async_copy(src, dst, sems.at[i]) for i, (src, dst) in enumerate(pairs)]
     for copy in copies:
         copy.start()
+    return copies
+
+
+def arrive(copies):
     for copy in copies:
         copy.wait()
 
@@ -65,17 +69,21 @@
 def outer_kernel(depth_ref, x_hbm, ter_hbm, o_ref, x_s, ter_s, rows_s, sems):
     row = iota(0, (8, S * L))
     groups = [(1, 1), (1, 2), (0, 0), (0, 3), (1, 0), (1, 3), (2, 0), (2, 3)]
-    fetch(
+    copies = fetch(
         [(ter_hbm.at[pl.ds(8, 16)], ter_s)]
         + [(x_hbm.at[f, pl.ds(8 * g, 8)], x_s.at[f, g]) for f, g in groups],
         sems,
     )
 
+    arrive(copies[:5])
+
     def flux(g):
         return lookup(ter_s[8 * g - 8 : 8 * g, :], depth_ref) * x_s[1, g]
 
     rows_s[0] = x_s[0, 0] - jnp.where(row == 7, 0.25 * pltpu.roll(flux(1), 7, 0), 0.0)
     rows_s[1] = x_s[0, 3] + jnp.where(row == 0, 0.25 * pltpu.roll(flux(2), 1, 0), 0.0)
+
+    arrive(copies[5:])
 
     def tile(q, c):
         cols = slice(L * c, L * c + L)
@@ -88,7 +96,7 @@
 
 def inner_kernel(x_hbm, o_ref, x_s, sems):
     groups = [(f, g) for f in range(F) for g in range(2)]
-    fetch([(x_hbm.at[f, pl.ds(8 * g + 8, 8)], x_s.at[f, g]) for f, g in groups], sems)
+    arrive(fetch([(x_hbm.at[f, pl.ds(8 * g + 8, 8)], x_s.at[f, g]) for f, g in groups], sems))
 
     def tile(q, c):
         return x_s[q % F, q // F, :, L * c : L * c + L]
@@ -328,7 +336,8 @@
 
 def unpack_kernel(x_ref, o_ref, sems):
     copies = [
-        pltpu.make_async_copy(x_ref.at[c], o_ref.at[:, :, pl.ds(L * c, L)], sems.at[c])
+        pltpu.make_async_copy(x_ref.at[c, f], o_ref.at[f, :, pl.ds(L * c, L)], sems.at[c, f])
+        for f in range(F)
         for c in range(S)
     ]
     for copy in copies:
@@ -448,7 +457,7 @@
         unpack_kernel,
         jax.ShapeDtypeStruct((F, rows, S * L), F32),
         (kept(parts),),
-        scratch=[pltpu.SemaphoreType.DMA((S,))],
+        scratch=[pltpu.SemaphoreType.DMA((S, F))],
         out_specs=pl.BlockSpec(memory_space=pl.ANY),
     )
     return gradient[None]

time: 68 us -> 68.3 us (level)
  no operation moved by 1% of the time
where the time goes in v6:
time: 68.3 us; the launch traced here: 67.9 us
  waiting for transfers between devices  19.4 us (28%)
  starting transfers between devices  19.1 us (28%)
  blocking collectives  16.3 us (24%)
  Pallas kernels  11.8 us (17%)
  local copies, waits for them, and re-layouts  0.99 us (1%)
    all_to_all x1, blocking collectives, local(): lax.all_to_all(mixed.reshape(S, F, rows, L), 'sub', split_axis=0, concat_...  16.3 us
    all_to_all x2, waiting for transfers between devices, to_chunks(): return lax.all_to_all(value, 'sub', split_axis=0, concat_axis=0, tiled=True)  14.1 us
    all_to_all x2, starting transfers between devices, to_chunks(): return lax.all_to_all(value, 'sub', split_axis=0, concat_axis=0, tiled=True)  9 us
    pallas_call x4, Pallas kernels, kernel(): pl.pallas_call(body, out_shape=out, in_specs=specs, out_specs=(out_specs,...  7.7 us
    ppermute x1, starting transfers between devices, local(): below = lax.ppermute(up, 'tile', back)  5.56 us
    ppermute x1, waiting for transfers between devices, local(): above = lax.ppermute(down, 'tile', forth)  4.84 us
    ppermute x1, starting transfers between devices, local(): above = lax.ppermute(down, 'tile', forth)  4.5 us
    pallas_call x1, Pallas kernels, local(): pl.pallas_call(outer_kernel, out_shape=pltpu.VMEM((S, NPART, 8, L), F32),...  2.79 us
  transfers between devices with their start and end apart: 4, of which 4 were waited for; matrix products, arithmetic and copies ran while one was open for 1% of the time, Pallas kernels for 3%

profile of v6, /device:TPU:256, one launch (start us, length us, event | category | flops | bytes accessed | tf_op | source)
XLA Modules:
  0.0 67.9 jit_solution(7826086116234425668)
XLA Ops:
  0.0 2.8 %shard_map.55 = f32[16,7,8,128]{3,2,1,0:T(8,128)} custom-call(f32[8]{0:T(128)} %depth_ref.3, f32[3,32,2048]{2,1,0:T(8,128)} %bitcast.16, s32[32,2048]{1,0:T(8,128)} %ter_ref.3), custom_call_target="tpu_custom_call" | custom-call | tf_op jit(solution)/shard_map/pallas_call | solution.py:384
  2.8 5.4 %all-to-all-start = ((f32[16,7,8,128]{3,2,1,0:T(8,128)}), f32[16,7,8,128]{3,2,1,0:T(8,128)S(1)}, u32[]{:S(2)}, u32[]{:S(2)}) async-start(f32[16,7,8,128]{3,2,1,0:T(8,128)} %shard_map.55), calls=%async_computation | async-start | bytes 917504 | tf_op jit(solution)/shard_map/all_to_all | solution.py:380
  8.2 0.0 copy-start.1
  8.3 1.3 %shard_map.56.x_ref = f32[16,7,8,128]{3,2,1,0:T(8,128)S(1)} custom-call(f32[3,32,2048]{2,1,0:T(8,128)} %bitcast.17), custom_call_target="tpu_custom_call" | custom-call | tf_op jit(solution)/shard_map/pallas_call | solution.py:402
  9.6 0.0 copy-start
  9.6 0.8 %copy-done = f32[16,7,8,128]{3,2,1,0:T(8,128)} copy-done((f32[16,7,8,128]{3,2,1,0:T(8,128)}, f32[16,7,8,128]{3,2,1,0:T(8,128)S(1)}, u32[]{:S(2)}) %copy-start) | copy-done | bytes 458776
  10.3 0.1 pad_add_fusion.place_ref
  10.4 8.0 %all-to-all-done.outer_ref = f32[16,7,8,128]{3,2,1,0:T(8,128)S(1)} async-done(((f32[16,7,8,128]{3,2,1,0:T(8,128)}), f32[16,7,8,128]{3,2,1,0:T(8,128)S(1)}, u32[]{:S(2)}, u32[]{:S(2)}) %all-to-all-start) | async-done | bytes 458784 | tf_op jit(solution)/shard_map/all_to_all | solution.py:380
  18.4 0.0 copy-done.1
  18.4 0.0 copy-start.5
  18.4 0.6 shard_map.57
  19.0 0.0 copy-start.2
  19.0 4.5 %collective-permute-start = (f32[57,8,128]{2,1,0:T(8,128)S(1)}, f32[57,8,128]{2,1,0:T(8,128)S(1)}, u32[]{:S(2)}, u32[]{:S(2)}) collective-permute-start(f32[57,8,128]{2,1,0:T(8,128)S(1)} %get-tuple-element.8), channel_id=1, source_target_pairs={{0,1},{1,2},{2,3},{3,4},{4,5},{5,6},{6,7},{7,8},{8,9},{9,10},{10,1... | collective-permute-start | bytes 700424 | tf_op jit(solution)/shard_map/ppermute | solution.py:400
  23.5 5.6 %collective-permute-start.1 = (f32[57,8,128]{2,1,0:T(8,128)S(1)}, f32[57,8,128]{2,1,0:T(8,128)S(1)}, u32[]{:S(2)}, u32[]{:S(2)}) collective-permute-start(f32[57,8,128]{2,1,0:T(8,128)S(1)} %get-tuple-element.7.after_ref), channel_id=1, source_target_pairs={{1,0},{2,1},{3,2},{4,3},{5,4},{6,5},{7,6},{8,7},{9,8},{10,9},{11,1... | collective-permute-start | bytes 700424 | tf_op jit(solution)/shard_map/ppermute | solution.py:401
  29.1 0.0 copy-done.5
  29.1 0.1 broadcast_multiply_fusion
  29.2 0.0 copy-done.2
  29.2 0.2 mul.31.weights_ref
  29.4 0.0 copy-start.3
  29.5 0.0 copy-start.4
  29.5 3.6 %all-to-all-start.1 = ((f32[16,7,8,128]{3,2,1,0:T(8,128)}), f32[16,7,8,128]{3,2,1,0:T(8,128)S(1)}, u32[]{:S(2)}, u32[]{:S(2)}) async-start(f32[16,7,8,128]{3,2,1,0:T(8,128)} %shard_map.58), calls=%async_computation.1 | async-start | bytes 917504 | tf_op jit(solution)/shard_map/all_to_all | solution.py:380
  33.1 4.8 %collective-permute-done.above_ref = f32[57,8,128]{2,1,0:T(8,128)S(1)} collective-permute-done((f32[57,8,128]{2,1,0:T(8,128)S(1)}, f32[57,8,128]{2,1,0:T(8,128)S(1)}, u32[]{:S(2)}, u32[]{:S(2)}) %collective-permute-start) | collective-permute-done | bytes 233504 | tf_op jit(solution)/shard_map/ppermute | solution.py:400
  37.9 0.5 collective-permute-done.1.below_ref
  38.4 0.0 copy-done.3
  38.4 0.0 copy-done.4
  38.4 1.0 %shard_map.59.coef_ref = f32[2,6,160,128]{3,2,1,0:T(8,128)S(1)} custom-call(s32[3]{0:T(128)S(1)} %pad_add_fusion.place_ref, f32[8]{0:T(128)S(1)} %copy-done.3, f32[8]{0:T(128)S(1)} %copy-done.4, s32[32,2048]{1,0:T(8,128)S(1)} %copy-done.1, f32[57,8,128]{2,1,0:T(8,128)S(1)} %collective-permute-done.above_ref, f32[57,8,128]{2,1,0:T(8,128)S(1)} %collective-permute-done.1.below_ref), custom_call_target="tpu_custom_call" | custom-call | flops 99999997952 | bytes 1000000 | tf_op jit(solution)/shard_map/pallas_call | solution.py:351
  39.4 6.1 %all-to-all-done.1 = f32[16,7,8,128]{3,2,1,0:T(8,128)S(1)} async-done(((f32[16,7,8,128]{3,2,1,0:T(8,128)}), f32[16,7,8,128]{3,2,1,0:T(8,128)S(1)}, u32[]{:S(2)}, u32[]{:S(2)}) %all-to-all-start.1) | async-done | bytes 458784 | tf_op jit(solution)/shard_map/all_to_all | solution.py:380
  45.5 4.8 %shard_map.60 = f32[1536,128]{1,0:T(8,128)S(1)} custom-call(s32[3]{0:T(128)S(1)} %pad_add_fusion.place_ref, f32[896,128]{1,0:T(8,128)S(1)} %bitcast.11, f32[896,128]{1,0:T(8,128)S(1)} %bitcast.13, f32[456,128]{1,0:T(8,128)S(1)} %bitcast.14, f32[456,128]{1,0:T(8,128)S(1)} %bitcast.15, f32[2,6,160,128]{3,2,1,0:T(8,128)S(1)} %shard_map.59.coef_ref, ...), custom_call_target="tpu_custom_call" | custom-call | tf_op jit(solution)/shard_map/pallas_call | solution.py:351
  50.3 16.3 %all_to_all.15.x_ref = f32[16,3,32,128]{3,2,1,0:T(8,128)S(1)} all-to-all(f32[16,3,32,128]{3,2,1,0:T(8,128)S(1)} %bitcast.12), channel_id=1, replica_groups=mesh['sub'=16,'tile'=32] {'sub'}, dimensions={0} | all-to-all | bytes 1572864 | tf_op jit(solution)/shard_map/all_to_all | solution.py:453
  66.6 1.3 %shard_map.61 = f32[3,32,2048]{2,1,0:T(8,128)} custom-call(f32[16,3,32,128]{3,2,1,0:T(8,128)S(1)} %all_to_all.15.x_ref), custom_call_target="tpu_custom_call" | custom-call | tf_op jit(solution)/shard_map/pallas_call | solution.py:351
  (2 shorter events, 0.0 us)
Async XLA Ops:
  2.8 15.6 %all-to-all-start = ((f32[16,7,8,128]{3,2,1,0:T(8,128)}), f32[16,7,8,128]{3,2,1,0:T(8,128)S(1)}, u32[]{:S(2)}, u32[]{:S(2)}) async-start(f32[16,7,8,128]{3,2,1,0:T(8,128)} %shard_map.55), calls=%async_computation | async-start | bytes 917504 | tf_op jit(solution)/shard_map/all_to_all | solution.py:380
  8.2 10.2 %copy-start.1 = (s32[32,2048]{1,0:T(8,128)S(1)}, s32[32,2048]{1,0:T(8,128)}, u32[]{:S(2)}) copy-start(s32[32,2048]{1,0:T(8,128)} %ter_ref.3) | copy-start | bytes 786436
  9.6 0.8 %copy-start = (f32[16,7,8,128]{3,2,1,0:T(8,128)}, f32[16,7,8,128]{3,2,1,0:T(8,128)S(1)}, u32[]{:S(2)}) copy-start(f32[16,7,8,128]{3,2,1,0:T(8,128)S(1)} %shard_map.56.x_ref) | copy-start | bytes 1376260
  18.4 10.7 %copy-start.5 = (f32[16,16]{1,0:T(8,128)S(1)}, f32[16,16]{1,0:T(8,128)}, u32[]{:S(2)}) copy-start(f32[16,16]{1,0:T(8,128)} %param.9) | copy-start | bytes 3076
  19.0 10.2 %copy-start.2 = (f32[57,8,128]{2,1,0:T(8,128)}, f32[57,8,128]{2,1,0:T(8,128)S(1)}, u32[]{:S(2)}) copy-start(f32[57,8,128]{2,1,0:T(8,128)S(1)} %get-tuple-element.7.after_ref) | copy-start | bytes 700420
  19.0 18.9 %collective-permute-start = (f32[57,8,128]{2,1,0:T(8,128)S(1)}, f32[57,8,128]{2,1,0:T(8,128)S(1)}, u32[]{:S(2)}, u32[]{:S(2)}) collective-permute-start(f32[57,8,128]{2,1,0:T(8,128)S(1)} %get-tuple-element.8), channel_id=1, source_target_pairs={{0,1},{1,2},{2,3},{3,4},{4,5},{5,6},{6,7},{7,8},{8,9},{9,10},{10,1... | collective-permute-start | bytes 700424 | tf_op jit(solution)/shard_map/ppermute | solution.py:400
  23.5 14.8 %collective-permute-start.1 = (f32[57,8,128]{2,1,0:T(8,128)S(1)}, f32[57,8,128]{2,1,0:T(8,128)S(1)}, u32[]{:S(2)}, u32[]{:S(2)}) collective-permute-start(f32[57,8,128]{2,1,0:T(8,128)S(1)} %get-tuple-element.7.after_ref), channel_id=1, source_target_pairs={{1,0},{2,1},{3,2},{4,3},{5,4},{6,5},{7,6},{8,7},{9,8},{10,9},{11,1... | collective-permute-start | bytes 700424 | tf_op jit(solution)/shard_map/ppermute | solution.py:401
  29.4 8.9 %copy-start.3 = (f32[8]{0:T(128)S(1)}, f32[8]{0:T(128)}, u32[]{:S(2)}) copy-start(f32[8]{0:T(128)} %depth_ref.3) | copy-start | bytes 100
  29.5 8.9 %copy-start.4 = (f32[8]{0:T(128)S(1)}, f32[8]{0:T(128)}, u32[]{:S(2)}) copy-start(f32[8]{0:T(128)} %spread_ref.1) | copy-start | bytes 100
  29.5 16.1 %all-to-all-start.1 = ((f32[16,7,8,128]{3,2,1,0:T(8,128)}), f32[16,7,8,128]{3,2,1,0:T(8,128)S(1)}, u32[]{:S(2)}, u32[]{:S(2)}) async-start(f32[16,7,8,128]{3,2,1,0:T(8,128)} %shard_map.58), calls=%async_computation.1 | async-start | bytes 917504 | tf_op jit(solution)/shard_map/all_to_all | solution.py:380
